TPU v7x, 512 devices: a whole 4x8x8 slice. The times are simulated.
512 devices in a mesh: blk: 32 (over z_lo, y), dp: 16 (over z_hi, x, core).
Axes of the slice: x: 4, y: 8, z: 8 (z_hi: 2, z_lo: 4; z = z_hi * 4 + z_lo), core: 2. Of those that a mesh axis runs over, the one named last changes fastest.
Arguments:
- queries: bfloat16 [16, 16384, 256], P('dp', 'blk'), may hold values from -8 to 8
- keys: bfloat16 [16, 1024, 256], P('dp', 'blk'), may hold values from -8 to 8
- events: bfloat16 [16, 1024, 4096], P('dp', 'blk'), may hold values from -6 to 6
- value_weight: bfloat16 [4096, 256], P('blk'), may hold values from -0.09375 to 0.09375
- attended_grad: bfloat16 [16, 16384, 256], P('dp', 'blk'), may hold values from -6 to 6
- note_patient: int32 [16, 16384], P('dp', 'blk'), may hold values from 0 to 7, never falling along the last dimension, each value on 1 to 4096 neighbouring positions
- event_patient: int32 [16, 1024], P('dp'), may hold values from 0 to 7, as said below
- block_lists: int32 [16, 128, 2], P('dp', 'blk'), may hold values from 0 to 7, all different within a row
Outputs:
- attended: bfloat16 [16, 16384, 256], P('dp', 'blk')
- query_grad: bfloat16 [16, 16384, 256], P('dp', 'blk')
- key_grad: bfloat16 [16, 1024, 256], P('dp', 'blk')
- event_grad: bfloat16 [16, 1024, 4096], P('dp', 'blk')
- weight_grad: float32 [4096, 256], P('blk')
Inputs may be any that keep to these rules, and one draw needn't show every extreme that they name: `note_patient`: patient numbers never fall along a batch's notes. `event_patient`: every aligned block of 128 events holds 16 events of each patient. `block_lists`: the 2 entries of a row name different event blocks; event block n holds events n * 128 to (n + 1) * 128 - 1.
All inputs are finite; a program needn't handle non-finite values.
Results may differ from a plain program's by a relative error of at most 0.03.
Values may be sent and summed in bfloat16 or wider, within the bound.
A program may use at most 64 MiB of HBM per device.

v0:
```python
import math

import jax
import jax.numpy as jnp
from jax import lax
from jax.sharding import PartitionSpec as P

DH = 128
H = 2
BLOCK = 128


masked_score = -1e30


def from_behind(value, axis, steps):
    count = lax.axis_size(axis)
    pairs = [(source, (source + steps) % count) for source in range(count)]
    return lax.ppermute(value, axis, pairs)


def shards(
    queries, keys, events, value_weight, attended_grad, note_patient, event_patient, block_lists
):
    cycle_size = lax.axis_size("blk")
    position = lax.axis_index("blk")
    event_rows = keys.shape[1]
    event_total = event_rows * cycle_size
    query_rows = queries.shape[1]
    head_width = queries.shape[2]
    event_blocks = event_total // BLOCK
    scale = 1.0 / math.sqrt(DH)
    query_heads = queries[0].reshape(query_rows, H, DH)
    grad_heads = attended_grad[0].reshape(query_rows, H, DH)
    own_keys = keys[0]
    my_events = events[0]
    full_weight = lax.all_gather(value_weight, "blk", axis=0, tiled=True)
    event_cols = lax.all_to_all(my_events, "blk", split_axis=1, concat_axis=0, tiled=True)
    own_values = jnp.dot(my_events, full_weight, preferred_element_type=jnp.float32).astype(
        jnp.bfloat16
    )
    block_ids = jnp.arange(event_blocks, dtype=jnp.int32)
    listed = jnp.any(block_lists[0][:, :, None] == block_ids[None, None, :], axis=1)
    listed_rows = jnp.repeat(listed.T.astype(jnp.float32), BLOCK, axis=1)
    my_patients = note_patient[0]
    all_patients = event_patient[0]

    def allowed(start, count):
        blocks = (start + jnp.arange(count, dtype=jnp.int32)) // BLOCK
        one_hot = (blocks[:, None] == block_ids[None, :]).astype(jnp.float32)
        hits = jnp.dot(one_hot, listed_rows)
        piece_patients = lax.dynamic_slice_in_dim(all_patients, start, count)
        return (hits > 0.5) & (piece_patients[:, None] == my_patients[None, :])

    def scores(key_piece):
        count = key_piece.shape[0]
        return (
            jnp.einsum(
                "jhd,ihd->hji",
                key_piece.reshape(count, H, DH),
                query_heads,
                preferred_element_type=jnp.float32,
            )
            * scale
        )

    start_state = (
        jnp.full((H, query_rows), masked_score, jnp.float32),
        jnp.zeros((H, query_rows), jnp.float32),
        jnp.zeros((query_rows, H, DH), jnp.float32),
    )
    key_piece = lax.all_gather(own_keys, "blk", axis=0, tiled=True)
    value_piece = lax.all_gather(own_values, "blk", axis=0, tiled=True)
    count = key_piece.shape[0]
    allow_mask = allowed(jnp.int32(0), count)

    def forward_compute(state):
        top_run, sum_run, output_run = state
        score = scores(key_piece)
        top_new = jnp.maximum(
            top_run, jnp.max(jnp.where(allow_mask[None], score, masked_score), axis=1)
        )
        weight = jnp.where(allow_mask[None], jnp.exp(score - top_new[:, None, :]), 0.0)
        fade = jnp.exp(top_run - top_new)
        sum_new = jnp.sum(weight, axis=1)
        mixed = jnp.einsum(
            "hji,jhd->ihd",
            weight.astype(jnp.bfloat16),
            value_piece.reshape(count, H, DH),
            preferred_element_type=jnp.float32,
        )
        return (top_new, sum_new, output_run * fade.T[:, :, None] + mixed)

    top_run, row_sum, output_run = lax.cond(
        jnp.any(allow_mask), forward_compute, lambda state: state, start_state
    )
    attended = (output_run / row_sum.T[:, :, None]).astype(jnp.bfloat16)
    log_total = top_run + jnp.log(row_sum)
    delta = jnp.sum(grad_heads.astype(jnp.float32) * attended.astype(jnp.float32), axis=2).T

    def grads_piece(query_sum, key_sum, value_sum, key_piece, value_piece, start):
        count = key_piece.shape[0]
        allow_mask = allowed(start, count)

        def grads_compute(state):
            query_run, key_run, value_run = state
            score = scores(key_piece)
            probability = jnp.where(allow_mask[None], jnp.exp(score - log_total[:, None, :]), 0.0)
            prob_grad = jnp.einsum(
                "jhd,ihd->hji",
                value_piece.reshape(count, H, DH),
                grad_heads,
                preferred_element_type=jnp.float32,
            )
            score_low = (probability * (prob_grad - delta[:, None, :])).astype(jnp.bfloat16)
            prob_low = probability.astype(jnp.bfloat16)
            query_run = query_run + jnp.einsum(
                "hji,jhd->ihd",
                score_low,
                key_piece.reshape(count, H, DH),
                preferred_element_type=jnp.float32,
            )
            key_run = key_run + jnp.einsum(
                "hji,ihd->jhd", score_low, query_heads, preferred_element_type=jnp.float32
            ).reshape(count, head_width)
            value_run = value_run + jnp.einsum(
                "hji,ihd->jhd", prob_low, grad_heads, preferred_element_type=jnp.float32
            ).reshape(count, head_width)
            return (query_run, key_run, value_run)

        return lax.cond(
            jnp.any(allow_mask), grads_compute, lambda state: state, (query_sum, key_sum, value_sum)
        )

    def visit(query_sum, state):
        key_piece, value_piece, key_sum, value_sum, source = state
        start = source * event_rows
        query_sum, key_sum, value_sum = grads_piece(
            query_sum, key_sum, value_sum, key_piece, value_piece, start
        )
        return (query_sum, (state[0], state[1], key_sum, value_sum, source))

    def step_up(state):
        key_piece, value_piece, key_sum, value_sum, source = state
        key_piece, value_piece = from_behind((key_piece, value_piece), "blk", 1)
        key_sum, value_sum = (
            from_behind(key_sum.astype(jnp.bfloat16), "blk", 1).astype(key_sum.dtype),
            from_behind(value_sum.astype(jnp.bfloat16), "blk", 1).astype(value_sum.dtype),
        )
        return (key_piece, value_piece, key_sum, value_sum, jnp.remainder(source - 1, cycle_size))

    zero_grads = jnp.zeros((event_rows, head_width), jnp.float32)
    query_sum = jnp.zeros((query_rows, H, DH), jnp.float32)
    home_state = (own_keys, own_values, zero_grads, zero_grads, position)
    query_sum, upward = visit(query_sum, home_state)
    reach_up = cycle_size - 1

    def one_way(index, carry):
        query_run, up_state = carry
        return visit(query_run, step_up(up_state))

    query_sum, upward = lax.fori_loop(0, reach_up, one_way, (query_sum, upward))
    back_down = (zero_grads, zero_grads)
    back_up = (
        from_behind(upward[2].astype(jnp.bfloat16), "blk", -reach_up % cycle_size).astype(
            jnp.float32
        ),
        from_behind(upward[3].astype(jnp.bfloat16), "blk", -reach_up % cycle_size).astype(
            jnp.float32
        ),
    )
    key_total = back_up[0] + back_down[0]
    value_total = back_up[1] + back_down[1]
    key_grad = (key_total * scale).astype(jnp.bfloat16)
    value_low = value_total.astype(jnp.bfloat16)
    event_grad = lax.dot_general(
        value_low, full_weight, (((1,), (1,)), ((), ())), preferred_element_type=jnp.float32
    ).astype(jnp.bfloat16)
    query_grad = (query_sum * scale).astype(jnp.bfloat16).reshape(query_rows, head_width)
    weight_share = lax.dot_general(
        event_cols,
        lax.all_gather(value_low, "blk", axis=0, tiled=True),
        (((0,), (0,)), ((), ())),
        preferred_element_type=jnp.float32,
    )
    weight_grad = lax.psum(weight_share.astype(jnp.bfloat16), "dp").astype(jnp.float32)
    return (
        attended.reshape(1, query_rows, head_width),
        query_grad[None],
        key_grad[None],
        event_grad[None],
        weight_grad,
    )


def solution(mesh):
    return jax.shard_map(
        shards,
        mesh=mesh,
        in_specs=(
            P("dp", "blk", None),
            P("dp", "blk", None),
            P("dp", "blk", None),
            P("blk", None),
            P("dp", "blk", None),
            P("dp", "blk"),
            P("dp", None),
            P("dp", "blk", None),
        ),
        out_specs=(
            P("dp", "blk", None),
            P("dp", "blk", None),
            P("dp", "blk", None),
            P("dp", "blk", None),
            P("blk", None),
        ),
        check_vma=False,
    )
```

profile of v0, /device:TPU:1, one launch (start us, length us, event | category | flops | bytes accessed | tf_op | source)
XLA Modules:
  0.0 1046.0 jit_solution(11387612145915857173)
XLA Ops:
  9.8 13.6 %all-to-all-start = ((bf16[32,32,128]{2,0,1:T(8,128)(2,1)}), bf16[32,32,128]{2,0,1:T(8,128)(2,1)S(1)}, u32[]{:S(2)}, u32[]{:S(2)}) async-start(bf16[32,32,128]{2,0,1:T(8,128)(2,1)} %copy.135), calls=%async_computation | async-start | bytes 524288 | tf_op jit(solution)/shard_map/all_to_all | solution.py:38
  25.5 2.4 fusion.65
  31.4 68.6 %all-gather = bf16[1,1024,256]{2,1,0:T(8,128)(2,1)S(1)} all-gather(bf16[1,32,256]{2,1,0:T(8,128)(2,1)S(1)} %copy.253), channel_id=2, replica_groups=mesh['blk'=32,'dp'=16] {'blk'}, dimensions={1}, use_global_device_ids=true | all-gather | bytes 540672 | tf_op jit(solution)/shard_map/all_gather | solution.py:72
  100.0 50.5 %all-gather.3.cloned.1.call-done = bf16[4096,256]{1,0:T(8,128)(2,1)} async-done(((bf16[128,256]{1,0:T(8,128)(2,1)}), bf16[4096,256]{1,0:T(8,128)(2,1)}) %all-gather.3.cloned.1.call-update) | async-done | bytes 2097168 | tf_op jit(solution)/shard_map/all_gather | solution.py:37
  150.5 2.1 convolution_convert_fusion.2
  152.5 66.7 %all_gather.14 = bf16[1024,256]{1,0:T(8,128)(2,1)S(1)} all-gather(bf16[32,256]{1,0:T(8,128)(2,1)S(1)} %convolution_convert_fusion.2), channel_id=1, replica_groups=mesh['blk'=32,'dp'=16] {'blk'}, dimensions={0}, use_global_device_ids=true | all-gather | bytes 540672 | tf_op jit(solution)/shard_map/all_gather | solution.py:73
  219.3 6.9 conditional.3
  220.8 2.3 fusion.5
  223.8 2.2 fusion.12
  228.5 468.9 %while.24 = (s32[]{:T(128)}, f32[512,2,128]{2,0,1:T(8,128)S(1)}, bf16[32,256]{1,0:T(8,128)(2,1)S(1)}, bf16[32,256]{1,0:T(8,128)(2,1)S(1)}, f32[32,256]{1,0:T(8,1...) while((s32[]{:T(128)}, f32[512,2,128]{2,0,1:T(8,128)S(1)}, ...), condition=%wide.region_14.15_spmd.clone, body=%wide.region_10.14_spmd.clone.sunk | while | flops 42681104 | bytes 3583314 | solution.py:162
  357.1 2.1 collective-permute-start.3
  371.3 2.5 collective-permute-start.3
  385.6 5.6 collective-permute-start.3
  394.0 2.9 collective-permute-start
  398.8 3.6 collective-permute-start.2
  402.4 4.2 collective-permute-start.3
  414.6 2.7 collective-permute-start.2
  417.3 5.7 collective-permute-start.3
  425.7 3.2 collective-permute-start
  430.9 2.3 collective-permute-start.2
  433.2 5.2 collective-permute-start.3
  441.6 2.8 collective-permute-start
  446.4 2.0 collective-permute-start.2
  448.4 5.3 collective-permute-start.3
  457.3 2.1 collective-permute-start
  461.3 2.2 collective-permute-start.2
  463.5 5.6 collective-permute-start.3
  471.9 2.8 collective-permute-start
  474.7 2.1 collective-permute-start.1
  478.7 4.2 collective-permute-start.3
  492.9 3.1 collective-permute-start.3
  507.1 2.5 collective-permute-start.3
  521.3 3.4 collective-permute-start.3
  535.5 6.1 collective-permute-start.3
  545.3 3.1 collective-permute-start
  548.5 2.0 collective-permute-start.1
  552.4 6.4 collective-permute-start.3
  564.4 2.1 collective-permute-start.1
  568.5 5.4 collective-permute-start.3
  583.8 4.7 collective-permute-start.3
  599.2 4.6 collective-permute-start.3
  614.5 2.3 collective-permute-start.3
  674.8 2.1 collective-permute-start.3
  689.0 5.7 collective-permute-start.3
  697.4 3.1 collective-permute-start.5
  703.5 3.1 collective-permute-start.4
  706.6 65.9 %all_gather.15 = bf16[1024,256]{1,0:T(8,128)(2,1)S(1)} all-gather(bf16[32,256]{1,0:T(8,128)(2,1)S(1)} %collective-permute-done.5), channel_id=1, replica_groups=mesh['blk'=32,'dp'=16] {'blk'}, dimensions={0}, use_global_device_ids=true | all-gather | bytes 540672 | tf_op jit(solution)/shard_map/all_gather | solution.py:182
  775.6 261.9 %all-reduce.2.cloned.1.call-done = bf16[128,256]{0,1:T(8,128)(2,1)} async-done(((bf16[128,256]{0,1:T(8,128)(2,1)}), bf16[128,256]{0,1:T(8,128)(2,1)}) %all-reduce.2.cloned.1.call-update) | async-done | bytes 65552 | tf_op jit(solution)/shard_map/psum | solution.py:186
  (701 shorter events, 358.3 us)
Async XLA Ops:
  7.2 143.3 %all-gather.3.cloned.1.call-start = ((), (), s32[]{:S(2)}) async-start(), calls=%async_computation.1 | async-start | bytes 2162688 | tf_op jit(solution)/shard_map/all_gather | solution.py:37
  9.8 762.7 %all-to-all-start = ((bf16[32,32,128]{2,0,1:T(8,128)(2,1)}), bf16[32,32,128]{2,0,1:T(8,128)(2,1)S(1)}, u32[]{:S(2)}, u32[]{:S(2)}) async-start(bf16[32,32,128]{2,0,1:T(8,128)(2,1)} %copy.135), calls=%async_computation | async-start | bytes 524288 | tf_op jit(solution)/shard_map/all_to_all | solution.py:38
  23.4 1014.1 %all-reduce.2.cloned.1.call-start = ((), (), s32[]{:S(2)}) async-start(), calls=%async_computation.2 | async-start | bytes 131072 | tf_op jit(solution)/shard_map/psum | solution.py:186
  228.5 10.1 collective-permute-start
  243.8 10.1 collective-permute-start
  259.2 10.1 collective-permute-start
  274.6 10.1 collective-permute-start
  289.9 10.1 collective-permute-start
  305.3 10.1 collective-permute-start
  351.3 10.3 collective-permute-start
  365.5 10.7 %collective-permute-start = (bf16[32,256]{1,0:T(8,128)(2,1)S(1)}, bf16[32,256]{1,0:T(8,128)(2,1)S(1)}, u32[]{:S(2)}, u32[]{:S(2)}) collective-permute-start(bf16[32,256]{1,0:T(8,128)(2,1)S(1)} %convert_element_type.166), channel_id=1, source_target_pairs={{0,16},{16,32},{32,48},{48,64},{64,80},{80,96},{96,112},{112,128},... | collective-permute-start | bytes 49160 | tf_op jit(solution)/shard_map/while/body/eval_jaxpr/ppermute | solution.py:19
  379.8 13.8 %collective-permute-start = (bf16[32,256]{1,0:T(8,128)(2,1)S(1)}, bf16[32,256]{1,0:T(8,128)(2,1)S(1)}, u32[]{:S(2)}, u32[]{:S(2)}) collective-permute-start(bf16[32,256]{1,0:T(8,128)(2,1)S(1)} %convert_element_type.166), channel_id=1, source_target_pairs={{0,16},{16,32},{32,48},{48,64},{64,80},{80,96},{96,112},{112,128},... | collective-permute-start | bytes 49160 | tf_op jit(solution)/shard_map/while/body/eval_jaxpr/ppermute | solution.py:19
  381.7 11.9 %collective-permute-start.1 = (bf16[32,256]{1,0:T(8,128)(2,1)S(1)}, bf16[32,256]{1,0:T(8,128)(2,1)S(1)}, u32[]{:S(2)}, u32[]{:S(2)}) collective-permute-start(bf16[32,256]{1,0:T(8,128)(2,1)S(1)} %convert_element_type.168), channel_id=1, source_target_pairs={{0,16},{16,32},{32,48},{48,64},{64,80},{80,96},{96,112},{112,128},... | collective-permute-start | bytes 49160 | tf_op jit(solution)/shard_map/while/body/eval_jaxpr/ppermute | solution.py:19
  394.0 15.0 %collective-permute-start = (bf16[32,256]{1,0:T(8,128)(2,1)S(1)}, bf16[32,256]{1,0:T(8,128)(2,1)S(1)}, u32[]{:S(2)}, u32[]{:S(2)}) collective-permute-start(bf16[32,256]{1,0:T(8,128)(2,1)S(1)} %convert_element_type.166), channel_id=1, source_target_pairs={{0,16},{16,32},{32,48},{48,64},{64,80},{80,96},{96,112},{112,128},... | collective-permute-start | bytes 49160 | tf_op jit(solution)/shard_map/while/body/eval_jaxpr/ppermute | solution.py:19
  396.9 12.1 %collective-permute-start.1 = (bf16[32,256]{1,0:T(8,128)(2,1)S(1)}, bf16[32,256]{1,0:T(8,128)(2,1)S(1)}, u32[]{:S(2)}, u32[]{:S(2)}) collective-permute-start(bf16[32,256]{1,0:T(8,128)(2,1)S(1)} %convert_element_type.168), channel_id=1, source_target_pairs={{0,16},{16,32},{32,48},{48,64},{64,80},{80,96},{96,112},{112,128},... | collective-permute-start | bytes 49160 | tf_op jit(solution)/shard_map/while/body/eval_jaxpr/ppermute | solution.py:19
  398.8 10.2 collective-permute-start.2
  410.8 14.6 %collective-permute-start = (bf16[32,256]{1,0:T(8,128)(2,1)S(1)}, bf16[32,256]{1,0:T(8,128)(2,1)S(1)}, u32[]{:S(2)}, u32[]{:S(2)}) collective-permute-start(bf16[32,256]{1,0:T(8,128)(2,1)S(1)} %convert_element_type.166), channel_id=1, source_target_pairs={{0,16},{16,32},{32,48},{48,64},{64,80},{80,96},{96,112},{112,128},... | collective-permute-start | bytes 49160 | tf_op jit(solution)/shard_map/while/body/eval_jaxpr/ppermute | solution.py:19
  412.7 12.7 %collective-permute-start.1 = (bf16[32,256]{1,0:T(8,128)(2,1)S(1)}, bf16[32,256]{1,0:T(8,128)(2,1)S(1)}, u32[]{:S(2)}, u32[]{:S(2)}) collective-permute-start(bf16[32,256]{1,0:T(8,128)(2,1)S(1)} %convert_element_type.168), channel_id=1, source_target_pairs={{0,16},{16,32},{32,48},{48,64},{64,80},{80,96},{96,112},{112,128},... | collective-permute-start | bytes 49160 | tf_op jit(solution)/shard_map/while/body/eval_jaxpr/ppermute | solution.py:19
  414.6 10.8 %collective-permute-start.2 = (bf16[32,256]{1,0:T(8,128)(2,1)S(1)}, bf16[32,256]{1,0:T(8,128)(2,1)S(1)}, u32[]{:S(2)}, u32[]{:S(2)}) collective-permute-start(bf16[32,256]{1,0:T(8,128)(2,1)S(1)} %get-tuple-element.678), channel_id=1, source_target_pairs={{0,16},{16,32},{32,48},{48,64},{64,80},{80,96},{96,112},{112,128},... | collective-permute-start | bytes 49160 | tf_op jit(solution)/shard_map/while/body/eval_jaxpr/ppermute | solution.py:19
  425.7 15.0 %collective-permute-start = (bf16[32,256]{1,0:T(8,128)(2,1)S(1)}, bf16[32,256]{1,0:T(8,128)(2,1)S(1)}, u32[]{:S(2)}, u32[]{:S(2)}) collective-permute-start(bf16[32,256]{1,0:T(8,128)(2,1)S(1)} %convert_element_type.166), channel_id=1, source_target_pairs={{0,16},{16,32},{32,48},{48,64},{64,80},{80,96},{96,112},{112,128},... | collective-permute-start | bytes 49160 | tf_op jit(solution)/shard_map/while/body/eval_jaxpr/ppermute | solution.py:19
  429.0 11.8 %collective-permute-start.1 = (bf16[32,256]{1,0:T(8,128)(2,1)S(1)}, bf16[32,256]{1,0:T(8,128)(2,1)S(1)}, u32[]{:S(2)}, u32[]{:S(2)}) collective-permute-start(bf16[32,256]{1,0:T(8,128)(2,1)S(1)} %convert_element_type.168), channel_id=1, source_target_pairs={{0,16},{16,32},{32,48},{48,64},{64,80},{80,96},{96,112},{112,128},... | collective-permute-start | bytes 49160 | tf_op jit(solution)/shard_map/while/body/eval_jaxpr/ppermute | solution.py:19
  441.6 14.5 %collective-permute-start = (bf16[32,256]{1,0:T(8,128)(2,1)S(1)}, bf16[32,256]{1,0:T(8,128)(2,1)S(1)}, u32[]{:S(2)}, u32[]{:S(2)}) collective-permute-start(bf16[32,256]{1,0:T(8,128)(2,1)S(1)} %convert_element_type.166), channel_id=1, source_target_pairs={{0,16},{16,32},{32,48},{48,64},{64,80},{80,96},{96,112},{112,128},... | collective-permute-start | bytes 49160 | tf_op jit(solution)/shard_map/while/body/eval_jaxpr/ppermute | solution.py:19
  444.5 11.6 %collective-permute-start.1 = (bf16[32,256]{1,0:T(8,128)(2,1)S(1)}, bf16[32,256]{1,0:T(8,128)(2,1)S(1)}, u32[]{:S(2)}, u32[]{:S(2)}) collective-permute-start(bf16[32,256]{1,0:T(8,128)(2,1)S(1)} %convert_element_type.168), channel_id=1, source_target_pairs={{0,16},{16,32},{32,48},{48,64},{64,80},{80,96},{96,112},{112,128},... | collective-permute-start | bytes 49160 | tf_op jit(solution)/shard_map/while/body/eval_jaxpr/ppermute | solution.py:19
  457.3 14.2 %collective-permute-start = (bf16[32,256]{1,0:T(8,128)(2,1)S(1)}, bf16[32,256]{1,0:T(8,128)(2,1)S(1)}, u32[]{:S(2)}, u32[]{:S(2)}) collective-permute-start(bf16[32,256]{1,0:T(8,128)(2,1)S(1)} %convert_element_type.166), channel_id=1, source_target_pairs={{0,16},{16,32},{32,48},{48,64},{64,80},{80,96},{96,112},{112,128},... | collective-permute-start | bytes 49160 | tf_op jit(solution)/shard_map/while/body/eval_jaxpr/ppermute | solution.py:19
  459.4 12.1 %collective-permute-start.1 = (bf16[32,256]{1,0:T(8,128)(2,1)S(1)}, bf16[32,256]{1,0:T(8,128)(2,1)S(1)}, u32[]{:S(2)}, u32[]{:S(2)}) collective-permute-start(bf16[32,256]{1,0:T(8,128)(2,1)S(1)} %convert_element_type.168), channel_id=1, source_target_pairs={{0,16},{16,32},{32,48},{48,64},{64,80},{80,96},{96,112},{112,128},... | collective-permute-start | bytes 49160 | tf_op jit(solution)/shard_map/while/body/eval_jaxpr/ppermute | solution.py:19
  461.3 10.2 collective-permute-start.2
  471.9 13.5 %collective-permute-start = (bf16[32,256]{1,0:T(8,128)(2,1)S(1)}, bf16[32,256]{1,0:T(8,128)(2,1)S(1)}, u32[]{:S(2)}, u32[]{:S(2)}) collective-permute-start(bf16[32,256]{1,0:T(8,128)(2,1)S(1)} %convert_element_type.166), channel_id=1, source_target_pairs={{0,16},{16,32},{32,48},{48,64},{64,80},{80,96},{96,112},{112,128},... | collective-permute-start | bytes 49160 | tf_op jit(solution)/shard_map/while/body/eval_jaxpr/ppermute | solution.py:19
  474.7 10.6 %collective-permute-start.1 = (bf16[32,256]{1,0:T(8,128)(2,1)S(1)}, bf16[32,256]{1,0:T(8,128)(2,1)S(1)}, u32[]{:S(2)}, u32[]{:S(2)}) collective-permute-start(bf16[32,256]{1,0:T(8,128)(2,1)S(1)} %convert_element_type.168), channel_id=1, source_target_pairs={{0,16},{16,32},{32,48},{48,64},{64,80},{80,96},{96,112},{112,128},... | collective-permute-start | bytes 49160 | tf_op jit(solution)/shard_map/while/body/eval_jaxpr/ppermute | solution.py:19
  487.1 11.3 %collective-permute-start = (bf16[32,256]{1,0:T(8,128)(2,1)S(1)}, bf16[32,256]{1,0:T(8,128)(2,1)S(1)}, u32[]{:S(2)}, u32[]{:S(2)}) collective-permute-start(bf16[32,256]{1,0:T(8,128)(2,1)S(1)} %convert_element_type.166), channel_id=1, source_target_pairs={{0,16},{16,32},{32,48},{48,64},{64,80},{80,96},{96,112},{112,128},... | collective-permute-start | bytes 49160 | tf_op jit(solution)/shard_map/while/body/eval_jaxpr/ppermute | solution.py:19
  501.3 10.7 %collective-permute-start = (bf16[32,256]{1,0:T(8,128)(2,1)S(1)}, bf16[32,256]{1,0:T(8,128)(2,1)S(1)}, u32[]{:S(2)}, u32[]{:S(2)}) collective-permute-start(bf16[32,256]{1,0:T(8,128)(2,1)S(1)} %convert_element_type.166), channel_id=1, source_target_pairs={{0,16},{16,32},{32,48},{48,64},{64,80},{80,96},{96,112},{112,128},... | collective-permute-start | bytes 49160 | tf_op jit(solution)/shard_map/while/body/eval_jaxpr/ppermute | solution.py:19
  515.5 11.6 %collective-permute-start = (bf16[32,256]{1,0:T(8,128)(2,1)S(1)}, bf16[32,256]{1,0:T(8,128)(2,1)S(1)}, u32[]{:S(2)}, u32[]{:S(2)}) collective-permute-start(bf16[32,256]{1,0:T(8,128)(2,1)S(1)} %convert_element_type.166), channel_id=1, source_target_pairs={{0,16},{16,32},{32,48},{48,64},{64,80},{80,96},{96,112},{112,128},... | collective-permute-start | bytes 49160 | tf_op jit(solution)/shard_map/while/body/eval_jaxpr/ppermute | solution.py:19
  529.7 14.3 %collective-permute-start = (bf16[32,256]{1,0:T(8,128)(2,1)S(1)}, bf16[32,256]{1,0:T(8,128)(2,1)S(1)}, u32[]{:S(2)}, u32[]{:S(2)}) collective-permute-start(bf16[32,256]{1,0:T(8,128)(2,1)S(1)} %convert_element_type.166), channel_id=1, source_target_pairs={{0,16},{16,32},{32,48},{48,64},{64,80},{80,96},{96,112},{112,128},... | collective-permute-start | bytes 49160 | tf_op jit(solution)/shard_map/while/body/eval_jaxpr/ppermute | solution.py:19
  531.7 12.4 %collective-permute-start.1 = (bf16[32,256]{1,0:T(8,128)(2,1)S(1)}, bf16[32,256]{1,0:T(8,128)(2,1)S(1)}, u32[]{:S(2)}, u32[]{:S(2)}) collective-permute-start(bf16[32,256]{1,0:T(8,128)(2,1)S(1)} %convert_element_type.168), channel_id=1, source_target_pairs={{0,16},{16,32},{32,48},{48,64},{64,80},{80,96},{96,112},{112,128},... | collective-permute-start | bytes 49160 | tf_op jit(solution)/shard_map/while/body/eval_jaxpr/ppermute | solution.py:19
  533.6 10.5 %collective-permute-start.2 = (bf16[32,256]{1,0:T(8,128)(2,1)S(1)}, bf16[32,256]{1,0:T(8,128)(2,1)S(1)}, u32[]{:S(2)}, u32[]{:S(2)}) collective-permute-start(bf16[32,256]{1,0:T(8,128)(2,1)S(1)} %get-tuple-element.678), channel_id=1, source_target_pairs={{0,16},{16,32},{32,48},{48,64},{64,80},{80,96},{96,112},{112,128},... | collective-permute-start | bytes 49160 | tf_op jit(solution)/shard_map/while/body/eval_jaxpr/ppermute | solution.py:19
  545.3 15.9 %collective-permute-start = (bf16[32,256]{1,0:T(8,128)(2,1)S(1)}, bf16[32,256]{1,0:T(8,128)(2,1)S(1)}, u32[]{:S(2)}, u32[]{:S(2)}) collective-permute-start(bf16[32,256]{1,0:T(8,128)(2,1)S(1)} %convert_element_type.166), channel_id=1, source_target_pairs={{0,16},{16,32},{32,48},{48,64},{64,80},{80,96},{96,112},{112,128},... | collective-permute-start | bytes 49160 | tf_op jit(solution)/shard_map/while/body/eval_jaxpr/ppermute | solution.py:19
  548.5 12.8 %collective-permute-start.1 = (bf16[32,256]{1,0:T(8,128)(2,1)S(1)}, bf16[32,256]{1,0:T(8,128)(2,1)S(1)}, u32[]{:S(2)}, u32[]{:S(2)}) collective-permute-start(bf16[32,256]{1,0:T(8,128)(2,1)S(1)} %convert_element_type.168), channel_id=1, source_target_pairs={{0,16},{16,32},{32,48},{48,64},{64,80},{80,96},{96,112},{112,128},... | collective-permute-start | bytes 49160 | tf_op jit(solution)/shard_map/while/body/eval_jaxpr/ppermute | solution.py:19
  550.5 10.8 %collective-permute-start.2 = (bf16[32,256]{1,0:T(8,128)(2,1)S(1)}, bf16[32,256]{1,0:T(8,128)(2,1)S(1)}, u32[]{:S(2)}, u32[]{:S(2)}) collective-permute-start(bf16[32,256]{1,0:T(8,128)(2,1)S(1)} %get-tuple-element.678), channel_id=1, source_target_pairs={{0,16},{16,32},{32,48},{48,64},{64,80},{80,96},{96,112},{112,128},... | collective-permute-start | bytes 49160 | tf_op jit(solution)/shard_map/while/body/eval_jaxpr/ppermute | solution.py:19
  562.5 13.8 %collective-permute-start = (bf16[32,256]{1,0:T(8,128)(2,1)S(1)}, bf16[32,256]{1,0:T(8,128)(2,1)S(1)}, u32[]{:S(2)}, u32[]{:S(2)}) collective-permute-start(bf16[32,256]{1,0:T(8,128)(2,1)S(1)} %convert_element_type.166), channel_id=1, source_target_pairs={{0,16},{16,32},{32,48},{48,64},{64,80},{80,96},{96,112},{112,128},... | collective-permute-start | bytes 49160 | tf_op jit(solution)/shard_map/while/body/eval_jaxpr/ppermute | solution.py:19
  564.4 11.9 %collective-permute-start.1 = (bf16[32,256]{1,0:T(8,128)(2,1)S(1)}, bf16[32,256]{1,0:T(8,128)(2,1)S(1)}, u32[]{:S(2)}, u32[]{:S(2)}) collective-permute-start(bf16[32,256]{1,0:T(8,128)(2,1)S(1)} %convert_element_type.168), channel_id=1, source_target_pairs={{0,16},{16,32},{32,48},{48,64},{64,80},{80,96},{96,112},{112,128},... | collective-permute-start | bytes 49160 | tf_op jit(solution)/shard_map/while/body/eval_jaxpr/ppermute | solution.py:19
  578.0 12.8 %collective-permute-start = (bf16[32,256]{1,0:T(8,128)(2,1)S(1)}, bf16[32,256]{1,0:T(8,128)(2,1)S(1)}, u32[]{:S(2)}, u32[]{:S(2)}) collective-permute-start(bf16[32,256]{1,0:T(8,128)(2,1)S(1)} %convert_element_type.166), channel_id=1, source_target_pairs={{0,16},{16,32},{32,48},{48,64},{64,80},{80,96},{96,112},{112,128},... | collective-permute-start | bytes 49160 | tf_op jit(solution)/shard_map/while/body/eval_jaxpr/ppermute | solution.py:19
  580.0 10.9 %collective-permute-start.1 = (bf16[32,256]{1,0:T(8,128)(2,1)S(1)}, bf16[32,256]{1,0:T(8,128)(2,1)S(1)}, u32[]{:S(2)}, u32[]{:S(2)}) collective-permute-start(bf16[32,256]{1,0:T(8,128)(2,1)S(1)} %convert_element_type.168), channel_id=1, source_target_pairs={{0,16},{16,32},{32,48},{48,64},{64,80},{80,96},{96,112},{112,128},... | collective-permute-start | bytes 49160 | tf_op jit(solution)/shard_map/while/body/eval_jaxpr/ppermute | solution.py:19
  593.4 12.7 %collective-permute-start = (bf16[32,256]{1,0:T(8,128)(2,1)S(1)}, bf16[32,256]{1,0:T(8,128)(2,1)S(1)}, u32[]{:S(2)}, u32[]{:S(2)}) collective-permute-start(bf16[32,256]{1,0:T(8,128)(2,1)S(1)} %convert_element_type.166), channel_id=1, source_target_pairs={{0,16},{16,32},{32,48},{48,64},{64,80},{80,96},{96,112},{112,128},... | collective-permute-start | bytes 49160 | tf_op jit(solution)/shard_map/while/body/eval_jaxpr/ppermute | solution.py:19
  595.3 10.8 %collective-permute-start.1 = (bf16[32,256]{1,0:T(8,128)(2,1)S(1)}, bf16[32,256]{1,0:T(8,128)(2,1)S(1)}, u32[]{:S(2)}, u32[]{:S(2)}) collective-permute-start(bf16[32,256]{1,0:T(8,128)(2,1)S(1)} %convert_element_type.168), channel_id=1, source_target_pairs={{0,16},{16,32},{32,48},{48,64},{64,80},{80,96},{96,112},{112,128},... | collective-permute-start | bytes 49160 | tf_op jit(solution)/shard_map/while/body/eval_jaxpr/ppermute | solution.py:19
  608.7 10.5 %collective-permute-start = (bf16[32,256]{1,0:T(8,128)(2,1)S(1)}, bf16[32,256]{1,0:T(8,128)(2,1)S(1)}, u32[]{:S(2)}, u32[]{:S(2)}) collective-permute-start(bf16[32,256]{1,0:T(8,128)(2,1)S(1)} %convert_element_type.166), channel_id=1, source_target_pairs={{0,16},{16,32},{32,48},{48,64},{64,80},{80,96},{96,112},{112,128},... | collective-permute-start | bytes 49160 | tf_op jit(solution)/shard_map/while/body/eval_jaxpr/ppermute | solution.py:19
  669.0 10.3 collective-permute-start
  683.2 13.9 %collective-permute-start = (bf16[32,256]{1,0:T(8,128)(2,1)S(1)}, bf16[32,256]{1,0:T(8,128)(2,1)S(1)}, u32[]{:S(2)}, u32[]{:S(2)}) collective-permute-start(bf16[32,256]{1,0:T(8,128)(2,1)S(1)} %convert_element_type.166), channel_id=1, source_target_pairs={{0,16},{16,32},{32,48},{48,64},{64,80},{80,96},{96,112},{112,128},... | collective-permute-start | bytes 49160 | tf_op jit(solution)/shard_map/while/body/eval_jaxpr/ppermute | solution.py:19
  685.1 11.9 %collective-permute-start.1 = (bf16[32,256]{1,0:T(8,128)(2,1)S(1)}, bf16[32,256]{1,0:T(8,128)(2,1)S(1)}, u32[]{:S(2)}, u32[]{:S(2)}) collective-permute-start(bf16[32,256]{1,0:T(8,128)(2,1)S(1)} %convert_element_type.168), channel_id=1, source_target_pairs={{0,16},{16,32},{32,48},{48,64},{64,80},{80,96},{96,112},{112,128},... | collective-permute-start | bytes 49160 | tf_op jit(solution)/shard_map/while/body/eval_jaxpr/ppermute | solution.py:19
  703.5 70.1 %collective-permute-start.4 = (bf16[32,256]{1,0:T(8,128)(2,1)S(1)}, bf16[32,256]{1,0:T(8,128)(2,1)S(1)}, u32[]{:S(2)}, u32[]{:S(2)}) collective-permute-start(bf16[32,256]{1,0:T(8,128)(2,1)S(1)} %convert_element_type.115), channel_id=1, source_target_pairs={{0,16},{16,32},{32,48},{48,64},{64,80},{80,96},{96,112},{112,128},... | collective-permute-start | bytes 49160 | tf_op jit(solution)/shard_map/ppermute | solution.py:19
  (85 other events, 963.4 us)
Sparse Core Ops, SparseCore 0:
  10.1 140.3 all-gather.2
  773.7 263.8 all-reduce.1
where the time goes:
time: 1050 us
  waiting for transfers between devices  391 us (37%)
  starting transfers between devices  315 us (30%)
  blocking collectives  201 us (19%)
  matrix products  53.4 us (5%)
  local copies, waits for them, and re-layouts  36.7 us (3%)
  loops' own time  24.8 us (2%)
  between operations  15.5 us (1%)
    ppermute x126, starting transfers between devices, from_behind(): return lax.ppermute(value, axis, pairs)  302 us
    psum x1, waiting for transfers between devices, shards(): lax.psum(weight_share.astype(jnp.bfloat16), 'dp').astype(jnp.float32)  262 us
    ppermute x126, waiting for transfers between devices, from_behind(): return lax.ppermute(value, axis, pairs)  78.6 us
    all_gather x1, blocking collectives, shards(): key_piece = lax.all_gather(own_keys, 'blk', axis=0, tiled=True)  68.6 us
    all_gather x1, blocking collectives, shards(): value_piece = lax.all_gather(own_values, 'blk', axis=0, tiled=True)  66.7 us
    all_gather x1, blocking collectives, shards(): lax.all_gather(value_low, 'blk', axis=0, tiled=True)  65.9 us
    all_gather x1, waiting for transfers between devices, shards(): full_weight = lax.all_gather(value_weight, 'blk', axis=0, tiled=True)  50.5 us
    dot_general x33, matrix products, allowed(): hits = jnp.dot(one_hot, listed_rows)  29.1 us
  transfers between devices with their start and end apart: 129, of which 60 were waited for; matrix products, arithmetic and copies ran while one was open for 9% of the time, Pallas kernels for 0%

commit v1 on v0

v1 whole, which is shorter than its diff:
```python
import functools
import math

import jax
import jax.numpy as jnp
from jax import lax
from jax.experimental import pallas as pl
from jax.experimental.pallas import tpu as pltpu
from jax.sharding import PartitionSpec as P

MESH = pl.DeviceIdType.MESH
DH = 128
BLOCK = 128
NZ, NY, NX = 4, 8, 4
masked_score = -1e30
scale = 1.0 / math.sqrt(DH)
f32 = jnp.float32
bf16 = jnp.bfloat16

Z_PEERS = [dict(dz=k) for k in (1, 3, 2)]
Y_STEPS = (4, 3, 5, 2, 6, 1, 7)
XC_PEERS = [dict(dx=a, dc=b) for a in (2, 1, 3, 0) for b in (0, 1) if (a, b) != (0, 0)]
ZH_PEERS = [dict(dzh=1, dx=a, dc=b) for a in (2, 1, 3, 0) for b in (0, 1)]


def place():
    blk = lax.axis_index("blk")
    dp = lax.axis_index("dp")
    return blk // NY, blk % NY, dp // 8, (dp // 2) % NX, dp % 2


def device(dz=0, dy=0, dzh=0, dx=0, dc=0):
    z, y, zh, x, c = place()
    return {
        "blk": lax.rem(z + dz, NZ) * NY + lax.rem(y + dy, NY),
        "dp": lax.rem(zh + dzh, 2) * 8 + lax.rem(x + dx, NX) * 2 + lax.rem(c + dc, 2),
    }


class Links:
    def __init__(self, send_sem, recv_sem):
        self.send_sem, self.recv_sem, self.count, self.started = send_sem, recv_sem, 0, []

    def push(self, src, dst, **to):
        index = self.count
        self.count += 1
        copy = pltpu.make_async_remote_copy(
            src_ref=src,
            dst_ref=dst,
            send_sem=self.send_sem.at[index],
            recv_sem=self.recv_sem.at[index],
            device_id=device(**to),
            device_id_type=MESH,
        )
        copy.start()
        self.started.append(copy)
        return copy

    def finish(self):
        for copy in self.started:
            copy.wait_send()


def arrive(copies):
    for copy in copies:
        copy.wait_recv()


def dot(a, b, ca, cb):
    return lax.dot_general(a, b, (((ca,), (cb,)), ((), ())), preferred_element_type=f32)


class Gather:
    def __init__(self, links, buf):
        self.links, self.buf = links, buf
        self.z, self.y = place()[:2]

    def first(self):
        z, y, buf = self.z, self.y, self.buf
        self.a1 = [self.links.push(buf[0].at[z, y], buf[0].at[z, y], **to) for to in Z_PEERS]
        self.b1 = [self.links.push(buf[1].at[z, y], buf[1].at[z, y], dy=k) for k in Y_STEPS]

    def second_a(self):
        arrive(self.a1)
        y, buf = self.y, self.buf
        self.a2 = [self.links.push(buf[0].at[:, y], buf[0].at[:, y], dy=k) for k in Y_STEPS]

    def second_b(self):
        arrive(self.b1)
        z, buf = self.z, self.buf
        self.b2 = [self.links.push(buf[1].at[z], buf[1].at[z], **to) for to in Z_PEERS]

    def done_a(self):
        arrive(self.a2)

    def done_b(self):
        arrive(self.b2)


class Scatter:
    def __init__(self, links, src, ra1, rb1, sa, sb, fa, fb, ra2, rb2):
        self.links, self.src, self.ra1, self.rb1 = links, src, ra1, rb1
        self.sa, self.sb, self.fa, self.fb, self.ra2, self.rb2 = sa, sb, fa, fb, ra2, rb2
        self.z, self.y = place()[:2]

    def first_a(self):
        self.a1 = [
            self.links.push(self.src.at[0, :, lax.rem(self.y + k, NY)], self.ra1.at[k - 1], dy=k)
            for k in Y_STEPS
        ]

    def first_b(self):
        self.b1 = [
            self.links.push(
                self.src.at[1, lax.rem(self.z + to["dz"], NZ)], self.rb1.at[to["dz"] - 1], **to
            )
            for to in Z_PEERS
        ]

    def second_a(self):
        arrive(self.a1)
        total = self.src[0, :, self.y].astype(f32)
        for k in range(NY - 1):
            total = total + self.ra1[k].astype(f32)
        self.fa[...] = total
        self.sa[...] = total.astype(bf16)
        self.a2 = [
            self.links.push(
                self.sa.at[lax.rem(self.z + to["dz"], NZ)], self.ra2.at[to["dz"] - 1], **to
            )
            for to in Z_PEERS
        ]

    def second_b(self):
        arrive(self.b1)
        total = self.src[1, self.z].astype(f32)
        for k in range(NZ - 1):
            total = total + self.rb1[k].astype(f32)
        self.fb[...] = total
        self.sb[...] = total.astype(bf16)
        self.b2 = [
            self.links.push(self.sb.at[lax.rem(self.y + k, NY)], self.rb2.at[k - 1], dy=k)
            for k in Y_STEPS
        ]

    def done_a(self):
        arrive(self.a2)
        total = self.fa[self.z]
        for k in range(NZ - 1):
            total = total + self.ra2[k].astype(f32)
        return total

    def done_b(self):
        arrive(self.b2)
        total = self.fb[self.y]
        for k in range(NY - 1):
            total = total + self.rb2[k].astype(f32)
        return total


def kernel(
    q_ref, k_ref, ev_ref, w_ref, g_ref, np_ref, ep_ref, bl_ref,
    att_ref, qg_ref, kg_ref, eg_ref, wg_ref,
    k0, k1, v0, v1, l0, l1, dvs, dks, wz, evz, pz, rz, ecols, egs, egr,
    ep8, probs, pd, sd, share, shb, sh2, r1, r2,
    va1, vb1, vsa, vsb, vfa, vfb, va2, vb2,
    ka1, kb1, ksa, ksb, kfa, kfb, ka2, kb2,
    send_sem, recv_sem,
):
    kall, vall, lall = (k0, k1), (v0, v1), (l0, l1)
    z, y, zh, x, c = place()
    part = x * 2 + c
    notes = q_ref.shape[1] // BLOCK
    barrier = pltpu.get_barrier_semaphore()
    peers = Z_PEERS + [dict(dy=k) for k in Y_STEPS] + XC_PEERS + ZH_PEERS
    for to in peers:
        pl.semaphore_signal(barrier, inc=1, device_id=device(**to), device_id_type=MESH)
    for h in range(2):
        kall[h][z, y] = k_ref[0, :, h * DH : (h + 1) * DH]
    wz[y] = w_ref[...]
    own_cols = pl.ds(pl.multiple_of(z * 1024, 1024), 1024)
    evz[z] = ev_ref[0, :, own_cols]
    for e in range(8):
        ep8[e : e + 1, :] = ep_ref[:, e * BLOCK : (e + 1) * BLOCK]
    pl.semaphore_wait(barrier, len(peers))

    links = Links(send_sem, recv_sem)
    keys = Gather(links, kall)
    keys.first()
    half = pl.ds(pl.multiple_of(c * 64, 64), 64)
    w1 = [links.push(wz.at[y, half], wz.at[y, half], dy=k) for k in Y_STEPS]
    ev1 = []
    for to in Z_PEERS:
        there = pl.ds(pl.multiple_of(lax.rem(z + to["dz"], NZ) * 1024, 1024), 1024)
        ev1.append(links.push(ev_ref.at[0, :, there], evz.at[z], **to))
    keys.second_a()
    keys.second_b()
    w2 = []
    for k, copy in zip(Y_STEPS, w1):
        copy.wait_recv()
        block = wz.at[lax.rem(y + NY - k, NY), half]
        w2.append(links.push(block, block, dc=1))
    arrive(ev1)
    arrive(w2)
    partial = dot(evz[...].reshape(128, 1024), wz[...].reshape(1024, 256), 1, 0)
    pz[...] = partial.reshape(NZ, 32, 256).astype(bf16)
    z1 = [
        links.push(pz.at[lax.rem(z + to["dz"], NZ)], rz.at[to["dz"] - 1], **to) for to in Z_PEERS
    ]
    spread = []
    for k in Y_STEPS:
        there = pl.ds(pl.multiple_of(lax.rem(y + k, NY) * 128, 128), 128)
        spread.append(links.push(evz.at[:, :, there], ecols.at[:, y], dy=k))
    ecols[:, y] = evz[:, :, pl.ds(pl.multiple_of(y * 128, 128), 128)]

    patients = []
    for n in range(notes):
        row = np_ref[:, n * BLOCK : (n + 1) * BLOCK]
        patients.append(jnp.broadcast_to(row, (BLOCK, BLOCK)).T)

    def chosen(buf, e):
        return buf[e // 2, pl.ds((e % 2) * 4, 4)].reshape(BLOCK, DH)

    def spread_out(dst, h, n, first, second):
        ids = (bl_ref[0, n, 0], bl_ref[0, n, 1])
        none = jnp.zeros_like(first)
        for e in range(8):
            tile = jnp.where(ids[0] == e, first, jnp.where(ids[1] == e, second, none))
            dst[h, n * BLOCK : (n + 1) * BLOCK, e * BLOCK : (e + 1) * BLOCK] = tile

    def head(h):
        return slice(h * DH, (h + 1) * DH)

    def score_head(h):
        for n in range(notes):
            q = q_ref[0, n * BLOCK : (n + 1) * BLOCK, head(h)]
            masked = []
            for slot in range(2):
                e = bl_ref[0, n, slot]
                s = dot(q, chosen(kall[h], e), 1, 1) * scale
                allow = patients[n] == ep8[pl.ds(e, 1), :]
                masked.append(jnp.where(allow, s, masked_score))
            top = jnp.max(jnp.maximum(masked[0], masked[1]), axis=1, keepdims=True)
            weight = [jnp.exp(s - top) for s in masked]
            row_sum = jnp.sum(weight[0] + weight[1], axis=1, keepdims=True)
            inverse = 1.0 / row_sum
            prob = [w * inverse for w in weight]
            for slot in range(2):
                probs[h, n, slot] = prob[slot]
            spread_out(pd, h, n, prob[0].astype(bf16), prob[1].astype(bf16))
        dvs[h] = dot(pd[h], g_ref[0, :, head(h)], 0, 0).astype(bf16).reshape(NZ, NY, 32, DH)

    def value_head(h):
        att = dot(pd[h], vall[h][...].reshape(1024, DH), 1, 0).astype(bf16)
        att_ref[0, :, head(h)] = att
        grad = g_ref[0, :, head(h)]
        delta = jnp.sum(grad.astype(f32) * att.astype(f32), axis=1, keepdims=True)
        for n in range(notes):
            rows = slice(n * BLOCK, (n + 1) * BLOCK)
            low = []
            for slot in range(2):
                pg = dot(grad[rows], chosen(vall[h], bl_ref[0, n, slot]), 1, 1)
                low.append((probs[h, n, slot] * (pg - delta[rows])).astype(bf16))
            spread_out(sd, h, n, low[0], low[1])
        dks[h] = dot(sd[h], q_ref[0, :, head(h)], 0, 0).astype(bf16).reshape(NZ, NY, 32, DH)

    def query_head(h):
        qg = dot(sd[h], kall[h][...].reshape(1024, DH), 1, 0) * scale
        qg_ref[0, :, head(h)] = qg.astype(bf16)

    value_sums = Scatter(links, dvs, va1, vb1, vsa, vsb, vfa, vfb, va2, vb2)
    key_sums = Scatter(links, dks, ka1, kb1, ksa, ksb, kfa, kfb, ka2, kb2)
    keys.done_a()
    score_head(0)
    value_sums.first_a()
    keys.done_b()
    score_head(1)
    value_sums.first_b()

    arrive(z1)
    own = pz[z].astype(f32)
    for k in range(NZ - 1):
        own = own + rz[k].astype(f32)
    for h in range(2):
        vall[h][z, y] = own[:, head(h)].astype(bf16)
    values = Gather(links, vall)
    values.first()
    value_sums.second_a()
    value_sums.second_b()
    values.second_a()
    values.second_b()
    l0[z, y] = value_sums.done_a().astype(bf16)
    l1[z, y] = value_sums.done_b().astype(bf16)
    lows = Gather(links, lall)
    lows.first()
    lows.second_a()
    lows.second_b()
    values.done_a()
    value_head(0)
    key_sums.first_a()
    values.done_b()
    value_head(1)
    key_sums.first_b()
    arrive(spread)
    lows.done_a()
    for h in range(2):
        if h == 1:
            lows.done_b()
        share[:, head(h)] = dot(ecols[...].reshape(1024, 128), lall[h][...].reshape(1024, DH), 0, 0)
    shb[...] = share[...].reshape(8, 16, 256).astype(bf16)
    x1 = []
    for i, to in enumerate(XC_PEERS):
        there = lax.rem(x + to["dx"], NX) * 2 + lax.rem(c + to["dc"], 2)
        x1.append(links.push(shb.at[there], r1.at[i], **to))
    low_rows = jnp.concatenate([lall[h][:, y].reshape(128, DH) for h in range(2)], axis=1)
    egs[...] = dot(low_rows, wz[...].reshape(1024, 256), 1, 1).astype(bf16).reshape(NZ, 32, 1024)
    e1 = [
        links.push(egs.at[lax.rem(z + to["dz"], NZ)], egr.at[z], **to) for to in Z_PEERS
    ]
    egr[z] = egs[z]
    arrive(x1)
    total = shb[part].astype(f32)
    for i in range(7):
        total = total + r1[i].astype(f32)
    sh2[...] = total.astype(bf16)
    x2 = [links.push(sh2, r2.at[zh, part], **to) for to in XC_PEERS + ZH_PEERS]
    r2[zh, part] = sh2[...]
    for h in range(2):
        query_head(h)
    key_sums.second_a()
    key_sums.second_b()
    arrive(e1)
    for k in range(NZ):
        eg_ref[0, :, k * 1024 : (k + 1) * 1024] = egr[k]
    kg_ref[0, :, head(0)] = (key_sums.done_a() * scale).astype(bf16)
    kg_ref[0, :, head(1)] = (key_sums.done_b() * scale).astype(bf16)
    arrive(x2)
    wg_ref[...] = (r2[0].astype(f32) + r2[1].astype(f32)).reshape(128, 256)
    links.finish()


def scatter_scratch():
    return [
        pltpu.VMEM((NY - 1, NZ, 32, DH), bf16),
        pltpu.VMEM((NZ - 1, NY, 32, DH), bf16),
        pltpu.VMEM((NZ, 32, DH), bf16),
        pltpu.VMEM((NY, 32, DH), bf16),
        pltpu.VMEM((NZ, 32, DH), f32),
        pltpu.VMEM((NY, 32, DH), f32),
        pltpu.VMEM((NZ - 1, 32, DH), bf16),
        pltpu.VMEM((NY - 1, 32, DH), bf16),
    ]


def shards(*args):
    def shape(s, t):
        return jax.ShapeDtypeStruct(s, t)

    vmem = pl.BlockSpec(memory_space=pltpu.VMEM)
    pair = pltpu.VMEM((2, NZ, NY, 32, DH), bf16)
    single = pltpu.VMEM((NZ, NY, 32, DH), bf16)
    return pl.pallas_call(
        kernel,
        out_shape=(
            shape((1, 512, 256), bf16),
            shape((1, 512, 256), bf16),
            shape((1, 32, 256), bf16),
            shape((1, 32, 4096), bf16),
            shape((128, 256), f32),
        ),
        in_specs=[vmem] * 7 + [pl.BlockSpec(memory_space=pltpu.SMEM)],
        out_specs=(vmem,) * 5,
        scratch_shapes=[single] * 6
        + [pair] * 2
        + [
            pltpu.VMEM((NY, 128, 256), bf16),
            pltpu.VMEM((NZ, 32, 1024), bf16),
            pltpu.VMEM((NZ, 32, 256), bf16),
            pltpu.VMEM((NZ - 1, 32, 256), bf16),
            pltpu.VMEM((NZ, NY, 32, 128), bf16),
            pltpu.VMEM((NZ, 32, 1024), bf16),
            pltpu.VMEM((NZ, 32, 1024), bf16),
            pltpu.VMEM((8, BLOCK), jnp.int32),
            pltpu.VMEM((2, 4, 2, BLOCK, BLOCK), f32),
            pltpu.VMEM((2, 512, 1024), bf16),
            pltpu.VMEM((2, 512, 1024), bf16),
            pltpu.VMEM((128, 256), f32),
            pltpu.VMEM((8, 16, 256), bf16),
            pltpu.VMEM((16, 256), bf16),
            pltpu.VMEM((7, 16, 256), bf16),
            pltpu.VMEM((2, 8, 16, 256), bf16),
        ]
        + scatter_scratch()
        + scatter_scratch()
        + [pltpu.SemaphoreType.DMA((160,)), pltpu.SemaphoreType.DMA((160,))],
        compiler_params=pltpu.CompilerParams(
            collective_id=0, has_side_effects=True, vmem_limit_bytes=40 * 1024 * 1024
        ),
        name="notes",
    )(*args)


def solution(mesh):
    return jax.shard_map(
        shards,
        mesh=mesh,
        in_specs=(
            P("dp", "blk", None),
            P("dp", "blk", None),
            P("dp", "blk", None),
            P("blk", None),
            P("dp", "blk", None),
            P("dp", "blk"),
            P("dp", None),
            P("dp", "blk", None),
        ),
        out_specs=(
            P("dp", "blk", None),
            P("dp", "blk", None),
            P("dp", "blk", None),
            P("dp", "blk", None),
            P("blk", None),
        ),
        check_vma=False,
    )
```

time: 1050 us -> 90.9 us (0.09)
  the two profiles are of different devices: /device:TPU:1 before, /device:TPU:8 now
where the time goes in v1:
time: 90.9 us; the launch traced here: 90.6 us
  Pallas kernels  80.7 us (89%)
  local copies, waits for them, and re-layouts  9.24 us (10%)
    pallas_call x1, Pallas kernels, shards(): pl.pallas_call(kernel, out_shape=(shape((1, 512, 256), bf16), shape((1, 5...  80.7 us
    unnamed x20, local copies, waits for them, and re-layouts  9.24 us

profile of v1, /device:TPU:8, one launch (start us, length us, event | category | flops | bytes accessed | tf_op | source)
XLA Modules:
  0.0 90.6 jit_solution(5919462797214148995)
XLA Ops:
  0.6 0.0 copy-start.6
  0.6 0.8 copy.13.bl_ref
  1.4 0.0 copy-done.6
  1.4 0.0 copy-start
  1.4 0.9 %copy-done = bf16[1,512,256]{2,1,0:T(8,128)(2,1)S(1)} copy-done((bf16[1,512,256]{2,1,0:T(8,128)(2,1)S(1)}, bf16[1,512,256]{2,1,0:T(8,128)(2,1)}, u32[]{:S(2)}) %copy-start) | copy-done | bytes 262168
  2.4 0.0 copy-start.1
  2.4 0.9 %copy-done.1 = bf16[1,32,4096]{2,1,0:T(8,128)(2,1)S(1)} copy-done((bf16[1,32,4096]{2,1,0:T(8,128)(2,1)S(1)}, bf16[1,32,4096]{2,1,0:T(8,128)(2,1)}, u32[]{:S(2)}) %copy-start.1) | copy-done | bytes 262168
  3.3 0.0 copy-start.2
  3.3 0.9 %copy-done.2 = bf16[1,512,256]{2,1,0:T(8,128)(2,1)S(1)} copy-done((bf16[1,512,256]{2,1,0:T(8,128)(2,1)S(1)}, bf16[1,512,256]{2,1,0:T(8,128)(2,1)}, u32[]{:S(2)}) %copy-start.2) | copy-done | bytes 262168
  4.3 0.0 copy-start.3
  4.3 0.8 copy-done.3
  5.1 0.0 copy-start.4
  5.1 0.7 copy-done.4
  5.8 0.0 copy-start.5
  5.8 0.7 copy-done.5
  6.5 80.7 %notes.1 = (bf16[1,512,256]{2,1,0:T(8,128)(2,1)S(1)}, bf16[1,512,256]{2,1,0:T(8,128)(2,1)S(1)}, bf16[1,32,256]{2,1,0:T(8,128)(2,1)S(1)}, bf16[1,32,4096]{2,1,0:T(8,128)(2,1)S(1)}, f32[128,256]{1,0:T(8,128)S(1)}) custom-call(bf16[1,512,256]{2,1,0:T(8,128)(2,1)S(1)} %copy-done, bf16[1,32,256]{2,1,0:T(8,128)(2,1)S(1)} %copy-done.4, ...), custom_call_target="tpu_custom_call" | custom-call | tf_op jit(solution)/shard_map/notes/pallas_call | solution.py:362
  87.2 0.7 copy.19
  87.9 0.7 copy.20
  88.6 0.6 copy.21
  89.2 0.7 copy.22
  89.9 0.7 copy.23
Async XLA Ops:
  0.6 0.8 copy-start.6
  1.4 1.0 %copy-start = (bf16[1,512,256]{2,1,0:T(8,128)(2,1)S(1)}, bf16[1,512,256]{2,1,0:T(8,128)(2,1)}, u32[]{:S(2)}) copy-start(bf16[1,512,256]{2,1,0:T(8,128)(2,1)} %q_ref.1) | copy-start | bytes 786436
  2.4 0.9 %copy-start.1 = (bf16[1,32,4096]{2,1,0:T(8,128)(2,1)S(1)}, bf16[1,32,4096]{2,1,0:T(8,128)(2,1)}, u32[]{:S(2)}) copy-start(bf16[1,32,4096]{2,1,0:T(8,128)(2,1)} %ev_ref.1) | copy-start | bytes 786436
  3.3 0.9 %copy-start.2 = (bf16[1,512,256]{2,1,0:T(8,128)(2,1)S(1)}, bf16[1,512,256]{2,1,0:T(8,128)(2,1)}, u32[]{:S(2)}) copy-start(bf16[1,512,256]{2,1,0:T(8,128)(2,1)} %g_ref.1) | copy-start | bytes 786436
  4.3 0.8 copy-start.3
  5.1 0.7 copy-start.4
  5.8 0.7 copy-start.5

commit v2 on v1

--- a/solution.py
+++ b/solution.py
@@ -56,6 +56,11 @@
         self.started.append(copy)
         return copy
 
+    def fetch(self, src, dst, sem):
+        copy = pltpu.make_async_copy(src, dst, sem)
+        copy.start()
+        return copy
+
     def finish(self):
         for copy in self.started:
             copy.wait_send()
@@ -159,15 +164,15 @@
 
 
 def kernel(
-    q_ref, k_ref, ev_ref, w_ref, g_ref, np_ref, ep_ref, bl_ref,
+    q_in, k_in, ev_in, w_in, g_in, np_in, ep_in, bl_in,
     att_ref, qg_ref, kg_ref, eg_ref, wg_ref,
-    k0, k1, v0, v1, l0, l1, dvs, dks, wz, evz, pz, rz, ecols, egs, egr,
-    ep8, probs, pd, sd, share, shb, sh2, r1, r2,
+    k0, k1, v0, v1, dvs, dks, wz, evz, pz, rz, egs, egr,
+    ep8, probs, pd, sd, lz0, lz1, pw, pr, xs, xr, ys, yr, sh2, r2,
     va1, vb1, vsa, vsb, vfa, vfb, va2, vb2,
     ka1, kb1, ksa, ksb, kfa, kfb, ka2, kb2,
-    send_sem, recv_sem,
+    q_ref, ev_ref, g_ref, np_ref, ep_ref, bl_ref, in_sem, send_sem, recv_sem,
 ):
-    kall, vall, lall = (k0, k1), (v0, v1), (l0, l1)
+    kall, vall = (k0, k1), (v0, v1)
     z, y, zh, x, c = place()
     part = x * 2 + c
     notes = q_ref.shape[1] // BLOCK
@@ -175,24 +180,42 @@
     peers = Z_PEERS + [dict(dy=k) for k in Y_STEPS] + XC_PEERS + ZH_PEERS
     for to in peers:
         pl.semaphore_signal(barrier, inc=1, device_id=device(**to), device_id_type=MESH)
-    for h in range(2):
-        kall[h][z, y] = k_ref[0, :, h * DH : (h + 1) * DH]
-    wz[y] = w_ref[...]
+    links = Links(send_sem, recv_sem)
     own_cols = pl.ds(pl.multiple_of(z * 1024, 1024), 1024)
-    evz[z] = ev_ref[0, :, own_cols]
-    for e in range(8):
-        ep8[e : e + 1, :] = ep_ref[:, e * BLOCK : (e + 1) * BLOCK]
+    loads = [
+        links.fetch(src, dst, in_sem.at[i])
+        for i, (src, dst) in enumerate(
+            [
+                (k_in.at[0, :, :DH], k0.at[z, y]),
+                (k_in.at[0, :, DH:], k1.at[z, y]),
+                (w_in, wz.at[y]),
+                (ev_in, ev_ref),
+                (ev_in.at[0, :, own_cols], evz.at[z]),
+                (q_in, q_ref),
+                (g_in, g_ref),
+                (np_in, np_ref),
+                (ep_in, ep_ref),
+                (bl_in, bl_ref),
+            ]
+        )
+    ]
     pl.semaphore_wait(barrier, len(peers))
-
-    links = Links(send_sem, recv_sem)
+    for load in loads[:2]:
+        load.wait()
     keys = Gather(links, kall)
     keys.first()
+    for load in loads[2:4]:
+        load.wait()
     half = pl.ds(pl.multiple_of(c * 64, 64), 64)
     w1 = [links.push(wz.at[y, half], wz.at[y, half], dy=k) for k in Y_STEPS]
     ev1 = []
     for to in Z_PEERS:
         there = pl.ds(pl.multiple_of(lax.rem(z + to["dz"], NZ) * 1024, 1024), 1024)
         ev1.append(links.push(ev_ref.at[0, :, there], evz.at[z], **to))
+    for load in loads[4:]:
+        load.wait()
+    for e in range(8):
+        ep8[e : e + 1, :] = ep_ref[:, e * BLOCK : (e + 1) * BLOCK]
     keys.second_a()
     keys.second_b()
     w2 = []
@@ -207,12 +230,6 @@
     z1 = [
         links.push(pz.at[lax.rem(z + to["dz"], NZ)], rz.at[to["dz"] - 1], **to) for to in Z_PEERS
     ]
-    spread = []
-    for k in Y_STEPS:
-        there = pl.ds(pl.multiple_of(lax.rem(y + k, NY) * 128, 128), 128)
-        spread.append(links.push(evz.at[:, :, there], ecols.at[:, y], dy=k))
-    ecols[:, y] = evz[:, :, pl.ds(pl.multiple_of(y * 128, 128), 128)]
-
     patients = []
     for n in range(notes):
         row = np_ref[:, n * BLOCK : (n + 1) * BLOCK]
@@ -222,7 +239,7 @@
         return buf[e // 2, pl.ds((e % 2) * 4, 4)].reshape(BLOCK, DH)
 
     def spread_out(dst, h, n, first, second):
-        ids = (bl_ref[0, n, 0], bl_ref[0, n, 1])
+        ids = (bl_ref[0, 0, n], bl_ref[0, 1, n])
         none = jnp.zeros_like(first)
         for e in range(8):
             tile = jnp.where(ids[0] == e, first, jnp.where(ids[1] == e, second, none))
@@ -236,7 +253,7 @@
             q = q_ref[0, n * BLOCK : (n + 1) * BLOCK, head(h)]
             masked = []
             for slot in range(2):
-                e = bl_ref[0, n, slot]
+                e = bl_ref[0, slot, n]
                 s = dot(q, chosen(kall[h], e), 1, 1) * scale
                 allow = patients[n] == ep8[pl.ds(e, 1), :]
                 masked.append(jnp.where(allow, s, masked_score))
@@ -259,7 +276,7 @@
             rows = slice(n * BLOCK, (n + 1) * BLOCK)
             low = []
             for slot in range(2):
-                pg = dot(grad[rows], chosen(vall[h], bl_ref[0, n, slot]), 1, 1)
+                pg = dot(grad[rows], chosen(vall[h], bl_ref[0, slot, n]), 1, 1)
                 low.append((probs[h, n, slot] * (pg - delta[rows])).astype(bf16))
             spread_out(sd, h, n, low[0], low[1])
         dks[h] = dot(sd[h], q_ref[0, :, head(h)], 0, 0).astype(bf16).reshape(NZ, NY, 32, DH)
@@ -267,7 +284,6 @@
     def query_head(h):
         qg = dot(sd[h], kall[h][...].reshape(1024, DH), 1, 0) * scale
         qg_ref[0, :, head(h)] = qg.astype(bf16)
-
     value_sums = Scatter(links, dvs, va1, vb1, vsa, vsb, vfa, vfb, va2, vb2)
     key_sums = Scatter(links, dks, ka1, kb1, ksa, ksb, kfa, kfb, ka2, kb2)
     keys.done_a()
@@ -276,7 +292,6 @@
     keys.done_b()
     score_head(1)
     value_sums.first_b()
-
     arrive(z1)
     own = pz[z].astype(f32)
     for k in range(NZ - 1):
@@ -289,39 +304,43 @@
     value_sums.second_b()
     values.second_a()
     values.second_b()
-    l0[z, y] = value_sums.done_a().astype(bf16)
-    l1[z, y] = value_sums.done_b().astype(bf16)
-    lows = Gather(links, lall)
-    lows.first()
-    lows.second_a()
-    lows.second_b()
+    lz0[z] = value_sums.done_a().astype(bf16)
+    low1 = []
+    low1 += [links.push(lz0.at[z], lz0.at[z], **to) for to in Z_PEERS]
+    lz1[z] = value_sums.done_b().astype(bf16)
+    low1 += [links.push(lz1.at[z], lz1.at[z], **to) for to in Z_PEERS]
     values.done_a()
     value_head(0)
     key_sums.first_a()
+    arrive(low1)
+    low_rows = jnp.concatenate([lz0[...].reshape(128, DH), lz1[...].reshape(128, DH)], axis=1)
+    c1 = []
+    for k in range(NY):
+        cols = evz[:, :, k * 128 : (k + 1) * 128].reshape(128, 128)
+        pw[k] = dot(cols, low_rows, 0, 0).astype(bf16).reshape(NX, 2, 16, 256)
+        c1.append(links.push(pw.at[k, :, 1 - c], pr.at[k], dc=1))
     values.done_b()
     value_head(1)
     key_sums.first_b()
-    arrive(spread)
-    lows.done_a()
-    for h in range(2):
-        if h == 1:
-            lows.done_b()
-        share[:, head(h)] = dot(ecols[...].reshape(1024, 128), lall[h][...].reshape(1024, DH), 0, 0)
-    shb[...] = share[...].reshape(8, 16, 256).astype(bf16)
-    x1 = []
-    for i, to in enumerate(XC_PEERS):
-        there = lax.rem(x + to["dx"], NX) * 2 + lax.rem(c + to["dc"], 2)
-        x1.append(links.push(shb.at[there], r1.at[i], **to))
-    low_rows = jnp.concatenate([lall[h][:, y].reshape(128, DH) for h in range(2)], axis=1)
+    for k in range(NY):
+        c1[k].wait_recv()
+        xs[k] = (pw[k, :, c].astype(f32) + pr[k].astype(f32)).astype(bf16)
+    x1 = [links.push(xs.at[:, lax.rem(x + k, NX)], xr.at[k - 1], dx=k) for k in (2, 1, 3)]
+    arrive(x1)
+    total = xs[:, x].astype(f32)
+    for k in range(NX - 1):
+        total = total + xr[k].astype(f32)
+    ys[...] = total.astype(bf16)
+    y1 = [links.push(ys.at[lax.rem(y + k, NY)], yr.at[k - 1], dy=k) for k in Y_STEPS]
     egs[...] = dot(low_rows, wz[...].reshape(1024, 256), 1, 1).astype(bf16).reshape(NZ, 32, 1024)
     e1 = [
         links.push(egs.at[lax.rem(z + to["dz"], NZ)], egr.at[z], **to) for to in Z_PEERS
     ]
     egr[z] = egs[z]
-    arrive(x1)
-    total = shb[part].astype(f32)
-    for i in range(7):
-        total = total + r1[i].astype(f32)
+    arrive(y1)
+    total = ys[y].astype(f32)
+    for k in range(NY - 1):
+        total = total + yr[k].astype(f32)
     sh2[...] = total.astype(bf16)
     x2 = [links.push(sh2, r2.at[zh, part], **to) for to in XC_PEERS + ZH_PEERS]
     r2[zh, part] = sh2[...]
@@ -352,6 +371,11 @@
     ]
 
 
+def hand_over(*refs):
+    for i in range(5):
+        refs[5 + i][...] = refs[i][...]
+
+
 def shards(*args):
     def shape(s, t):
         return jax.ShapeDtypeStruct(s, t)
@@ -359,7 +383,7 @@
     vmem = pl.BlockSpec(memory_space=pltpu.VMEM)
     pair = pltpu.VMEM((2, NZ, NY, 32, DH), bf16)
     single = pltpu.VMEM((NZ, NY, 32, DH), bf16)
-    return pl.pallas_call(
+    results = pl.pallas_call(
         kernel,
         out_shape=(
             shape((1, 512, 256), bf16),
@@ -368,36 +392,54 @@
             shape((1, 32, 4096), bf16),
             shape((128, 256), f32),
         ),
-        in_specs=[vmem] * 7 + [pl.BlockSpec(memory_space=pltpu.SMEM)],
+        in_specs=[pl.BlockSpec(memory_space=pl.ANY)] * 8,
         out_specs=(vmem,) * 5,
-        scratch_shapes=[single] * 6
+        scratch_shapes=[single] * 4
         + [pair] * 2
         + [
             pltpu.VMEM((NY, 128, 256), bf16),
             pltpu.VMEM((NZ, 32, 1024), bf16),
             pltpu.VMEM((NZ, 32, 256), bf16),
             pltpu.VMEM((NZ - 1, 32, 256), bf16),
-            pltpu.VMEM((NZ, NY, 32, 128), bf16),
             pltpu.VMEM((NZ, 32, 1024), bf16),
             pltpu.VMEM((NZ, 32, 1024), bf16),
             pltpu.VMEM((8, BLOCK), jnp.int32),
             pltpu.VMEM((2, 4, 2, BLOCK, BLOCK), f32),
             pltpu.VMEM((2, 512, 1024), bf16),
             pltpu.VMEM((2, 512, 1024), bf16),
-            pltpu.VMEM((128, 256), f32),
-            pltpu.VMEM((8, 16, 256), bf16),
+            pltpu.VMEM((NZ, 32, DH), bf16),
+            pltpu.VMEM((NZ, 32, DH), bf16),
+            pltpu.VMEM((NY, NX, 2, 16, 256), bf16),
+            pltpu.VMEM((NY, NX, 16, 256), bf16),
+            pltpu.VMEM((NY, NX, 16, 256), bf16),
+            pltpu.VMEM((NX - 1, NY, 16, 256), bf16),
+            pltpu.VMEM((NY, 16, 256), bf16),
+            pltpu.VMEM((NY - 1, 16, 256), bf16),
             pltpu.VMEM((16, 256), bf16),
-            pltpu.VMEM((7, 16, 256), bf16),
             pltpu.VMEM((2, 8, 16, 256), bf16),
         ]
         + scatter_scratch()
         + scatter_scratch()
+        + [
+            pltpu.VMEM((1, 512, 256), bf16),
+            pltpu.VMEM((1, 32, 4096), bf16),
+            pltpu.VMEM((1, 512, 256), bf16),
+            pltpu.VMEM((1, 512), jnp.int32),
+            pltpu.VMEM((1, 1024), jnp.int32),
+            pltpu.SMEM((1, 2, 4), jnp.int32),
+            pltpu.SemaphoreType.DMA((10,)),
+        ]
         + [pltpu.SemaphoreType.DMA((160,)), pltpu.SemaphoreType.DMA((160,))],
         compiler_params=pltpu.CompilerParams(
-            collective_id=0, has_side_effects=True, vmem_limit_bytes=40 * 1024 * 1024
+            collective_id=0, has_side_effects=True, vmem_limit_bytes=60 * 1024 * 1024
         ),
         name="notes",
-    )(*args)
+    )(*args[:7], jnp.swapaxes(args[7], 1, 2))
+    return pl.pallas_call(
+        hand_over,
+        out_shape=tuple(shape(r.shape, r.dtype) for r in results),
+        name="hand_over",
+    )(*results)
 
 
 def solution(mesh):

time: 90.9 us -> 77.4 us (0.85)
  the two profiles are of different devices: /device:TPU:8 before, /device:TPU:1 now
where the time goes in v2:
time: 77.4 us; the launch traced here: 77.3 us
  Pallas kernels  76.6 us (99%)
    pallas_call x1, Pallas kernels, shards(): pl.pallas_call(kernel, out_shape=(shape((1, 512, 256), bf16), shape((1, 5...  74.5 us
    pallas_call x1, Pallas kernels, shards(): pl.pallas_call(hand_over, out_shape=tuple((shape(r.shape, r.dtype) for r...  2.1 us

profile of v2, /device:TPU:1, one launch (start us, length us, event | category | flops | bytes accessed | tf_op | source)
XLA Modules:
  0.0 77.3 jit_solution(7992310038975953982)
XLA Ops:
  0.6 74.5 %notes.1 = (bf16[1,512,256]{2,1,0:T(8,128)(2,1)}, bf16[1,512,256]{2,1,0:T(8,128)(2,1)}, bf16[1,32,256]{2,1,0:T(8,128)(2,1)}, bf16[1,32,4096]{2,1,0:T(8,128)(2,1)}, f32[128,256]{1,0:T(8,128)}) custom-call(bf16[1,512,256]{2,1,0:T(8,128)(2,1)} %q_in.1, bf16[1,32,256]{2,1,0:T(8,128)(2,1)} %k_in.1, bf16[1,32,4096]{2,1,0:T(8,128)(2,1)} %ev_in.1, ...), custom_call_target="tpu_custom_call" | custom-call | tf_op jit(solution)/shard_map/notes/pallas_call | solution.py:386
  75.2 2.1 %hand_over.1 = (bf16[1,512,256]{2,1,0:T(8,128)(2,1)}, bf16[1,512,256]{2,1,0:T(8,128)(2,1)}, bf16[1,32,256]{2,1,0:T(8,128)(2,1)}, bf16[1,32,4096]{2,1,0:T(8,128)(2,1)}, f32[128,256]{1,0:T(8,128)}) custom-call(bf16[1,512,256]{2,1,0:T(8,128)(2,1)} %get-tuple-element.10.refs_0_, bf16[1,512,256]{2,1,0:T(8,128)(2,1)} %get-tuple-element.11.refs_1_, ...), custom_call_target="tpu_custom_call" | custom-call | tf_op jit(solution)/shard_map/hand_over/pallas_call | solution.py:438

commit v3 on v2

--- a/solution.py
+++ b/solution.py
@@ -20,7 +20,7 @@
 Z_PEERS = [dict(dz=k) for k in (1, 3, 2)]
 Y_STEPS = (4, 3, 5, 2, 6, 1, 7)
 XC_PEERS = [dict(dx=a, dc=b) for a in (2, 1, 3, 0) for b in (0, 1) if (a, b) != (0, 0)]
-ZH_PEERS = [dict(dzh=1, dx=a, dc=b) for a in (2, 1, 3, 0) for b in (0, 1)]
+ZH_PEERS = [dict(dzh=1)]
 
 
 def place():
@@ -80,13 +80,15 @@
         self.links, self.buf = links, buf
         self.z, self.y = place()[:2]
 
-    def first(self):
+    def first_a(self):
         z, y, buf = self.z, self.y, self.buf
         self.a1 = [self.links.push(buf[0].at[z, y], buf[0].at[z, y], **to) for to in Z_PEERS]
+
+    def first_b(self):
+        z, y, buf = self.z, self.y, self.buf
         self.b1 = [self.links.push(buf[1].at[z, y], buf[1].at[z, y], dy=k) for k in Y_STEPS]
 
     def second_a(self):
-        arrive(self.a1)
         y, buf = self.y, self.buf
         self.a2 = [self.links.push(buf[0].at[:, y], buf[0].at[:, y], dy=k) for k in Y_STEPS]
 
@@ -122,7 +124,7 @@
             for to in Z_PEERS
         ]
 
-    def second_a(self):
+    def second_a(self, whole=False):
         arrive(self.a1)
         total = self.src[0, :, self.y].astype(f32)
         for k in range(NY - 1):
@@ -131,7 +133,9 @@
         self.sa[...] = total.astype(bf16)
         self.a2 = [
             self.links.push(
-                self.sa.at[lax.rem(self.z + to["dz"], NZ)], self.ra2.at[to["dz"] - 1], **to
+                self.sa if whole else self.sa.at[lax.rem(self.z + to["dz"], NZ)],
+                self.ra2.at[to["dz"] - 1],
+                **to,
             )
             for to in Z_PEERS
         ]
@@ -148,9 +152,9 @@
             for k in Y_STEPS
         ]
 
-    def done_a(self):
+    def done_a(self, whole=False):
         arrive(self.a2)
-        total = self.fa[self.z]
+        total = self.fa[...] if whole else self.fa[self.z]
         for k in range(NZ - 1):
             total = total + self.ra2[k].astype(f32)
         return total
@@ -165,19 +169,19 @@
 
 def kernel(
     q_in, k_in, ev_in, w_in, g_in, np_in, ep_in, bl_in,
-    att_ref, qg_ref, kg_ref, eg_ref, wg_ref,
-    k0, k1, v0, v1, dvs, dks, wz, evz, pz, rz, egs, egr,
-    ep8, probs, pd, sd, lz0, lz1, pw, pr, xs, xr, ys, yr, sh2, r2,
+    att_out, qg_out, kg_out, eg_out, wg_out,
+    k0, k1, v0, v1, dvs, dks, wq, wz, evz, pz0, pz1, rz0, rz1, evt, egs, egr,
+    ep8, probs, pd, sd, lz0, lz1, pw, pr, xs, xr, ys, yr, sh2, rzh, sh3, r2,
     va1, vb1, vsa, vsb, vfa, vfb, va2, vb2,
     ka1, kb1, ksa, ksb, kfa, kfb, ka2, kb2,
-    q_ref, ev_ref, g_ref, np_ref, ep_ref, bl_ref, in_sem, send_sem, recv_sem,
+    q_ref, ev_ref, g_ref, np_ref, ep_ref, bl_ref, att_ref, qg_ref, kg_ref, in_sem, out_sem, send_sem, recv_sem,
 ):
     kall, vall = (k0, k1), (v0, v1)
     z, y, zh, x, c = place()
     part = x * 2 + c
     notes = q_ref.shape[1] // BLOCK
     barrier = pltpu.get_barrier_semaphore()
-    peers = Z_PEERS + [dict(dy=k) for k in Y_STEPS] + XC_PEERS + ZH_PEERS
+    peers = ZH_PEERS + [dict(dy=k) for k in Y_STEPS] + Z_PEERS + XC_PEERS
     for to in peers:
         pl.semaphore_signal(barrier, inc=1, device_id=device(**to), device_id_type=MESH)
     links = Links(send_sem, recv_sem)
@@ -188,7 +192,7 @@
             [
                 (k_in.at[0, :, :DH], k0.at[z, y]),
                 (k_in.at[0, :, DH:], k1.at[z, y]),
-                (w_in, wz.at[y]),
+                (w_in.at[pl.ds(pl.multiple_of(part * 16, 16), 16)], wq.at[x, c, y]),
                 (ev_in, ev_ref),
                 (ev_in.at[0, :, own_cols], evz.at[z]),
                 (q_in, q_ref),
@@ -200,14 +204,14 @@
         )
     ]
     pl.semaphore_wait(barrier, len(peers))
+    for load in loads[2:4]:
+        load.wait()
+    w1 = [links.push(wq.at[x, c, y], wq.at[x, c, y], dy=k) for k in Y_STEPS]
     for load in loads[:2]:
         load.wait()
     keys = Gather(links, kall)
-    keys.first()
-    for load in loads[2:4]:
-        load.wait()
-    half = pl.ds(pl.multiple_of(c * 64, 64), 64)
-    w1 = [links.push(wz.at[y, half], wz.at[y, half], dy=k) for k in Y_STEPS]
+    keys.first_a()
+    keys.first_b()
     ev1 = []
     for to in Z_PEERS:
         there = pl.ds(pl.multiple_of(lax.rem(z + to["dz"], NZ) * 1024, 1024), 1024)
@@ -216,19 +220,31 @@
         load.wait()
     for e in range(8):
         ep8[e : e + 1, :] = ep_ref[:, e * BLOCK : (e + 1) * BLOCK]
+    arrive(w1)
+    w2 = [links.push(wq.at[x, c], wq.at[x, c], dx=k) for k in (2, 1, 3)]
+    w3 = [links.push(wq.at[x, c], wq.at[x, c], dc=1)]
+    arrive(keys.a1)
     keys.second_a()
     keys.second_b()
-    w2 = []
-    for k, copy in zip(Y_STEPS, w1):
+    for k, copy in zip((2, 1, 3), w2):
         copy.wait_recv()
-        block = wz.at[lax.rem(y + NY - k, NY), half]
-        w2.append(links.push(block, block, dc=1))
+        block = wq.at[lax.rem(x + NX - k, NX), c]
+        w3.append(links.push(block, block, dc=1))
     arrive(ev1)
-    arrive(w2)
+    arrive(w3)
+    for a in range(NX):
+        for b in range(2):
+            for k in range(NY):
+                low = (a * 2 + b) * 16
+                wz[k, low : low + 16] = wq[a, b, k]
     partial = dot(evz[...].reshape(128, 1024), wz[...].reshape(1024, 256), 1, 0)
-    pz[...] = partial.reshape(NZ, 32, 256).astype(bf16)
-    z1 = [
-        links.push(pz.at[lax.rem(z + to["dz"], NZ)], rz.at[to["dz"] - 1], **to) for to in Z_PEERS
+    pz0[...] = partial[:, :DH].reshape(NZ, 32, DH).astype(bf16)
+    pz1[...] = partial[:, DH:].reshape(NZ, 32, DH).astype(bf16)
+    z1a = [
+        links.push(pz0.at[lax.rem(z + to["dz"], NZ)], rz0.at[to["dz"] - 1], **to) for to in Z_PEERS
+    ]
+    z1b = [
+        links.push(pz1.at[lax.rem(z + to["dz"], NZ)], rz1.at[to["dz"] - 1], **to) for to in Z_PEERS
     ]
     patients = []
     for n in range(notes):
@@ -247,6 +263,23 @@
 
     def head(h):
         return slice(h * DH, (h + 1) * DH)
+
+    handed = []
+
+    def hand(src, dst):
+        handed.append(links.fetch(src, dst, out_sem.at[len(handed)]))
+
+    def share_head(h):
+        low = (lz0, lz1)[h][...].reshape(128, DH)
+        pw[h] = dot(evt[...], low, 1, 0).astype(bf16).reshape(NY, NX, 2, 16, DH)
+        return links.push(pw.at[h, :, :, 1 - c], pr.at[h], dc=1)
+
+    def sum_head(h, copy):
+        copy.wait_recv()
+        xs[h] = (pw[h, :, :, c].astype(f32) + pr[h].astype(f32)).astype(bf16)
+        return [
+            links.push(xs.at[h, :, lax.rem(x + k, NX)], xr.at[h, k - 1], dx=k) for k in (2, 1, 3)
+        ]
 
     def score_head(h):
         for n in range(notes):
@@ -292,73 +325,82 @@
     keys.done_b()
     score_head(1)
     value_sums.first_b()
-    arrive(z1)
-    own = pz[z].astype(f32)
+    values = Gather(links, vall)
+    arrive(z1a)
+    own = pz0[z].astype(f32)
     for k in range(NZ - 1):
-        own = own + rz[k].astype(f32)
-    for h in range(2):
-        vall[h][z, y] = own[:, head(h)].astype(bf16)
-    values = Gather(links, vall)
-    values.first()
-    value_sums.second_a()
+        own = own + rz0[k].astype(f32)
+    v0[z, y] = own.astype(bf16)
+    values.first_a()
+    arrive(z1b)
+    own = pz1[z].astype(f32)
+    for k in range(NZ - 1):
+        own = own + rz1[k].astype(f32)
+    v1[z, y] = own.astype(bf16)
+    values.first_b()
+    evt[...] = evz[...].reshape(128, 1024).T
+    value_sums.second_a(whole=True)
     value_sums.second_b()
+    arrive(values.a1)
     values.second_a()
     values.second_b()
-    lz0[z] = value_sums.done_a().astype(bf16)
-    low1 = []
-    low1 += [links.push(lz0.at[z], lz0.at[z], **to) for to in Z_PEERS]
     lz1[z] = value_sums.done_b().astype(bf16)
-    low1 += [links.push(lz1.at[z], lz1.at[z], **to) for to in Z_PEERS]
+    low1 = [links.push(lz1.at[z], lz1.at[z], **to) for to in Z_PEERS]
+    lz0[...] = value_sums.done_a(whole=True).astype(bf16)
+    c10 = share_head(0)
+    x10 = sum_head(0, c10)
     values.done_a()
     value_head(0)
     key_sums.first_a()
     arrive(low1)
-    low_rows = jnp.concatenate([lz0[...].reshape(128, DH), lz1[...].reshape(128, DH)], axis=1)
-    c1 = []
-    for k in range(NY):
-        cols = evz[:, :, k * 128 : (k + 1) * 128].reshape(128, 128)
-        pw[k] = dot(cols, low_rows, 0, 0).astype(bf16).reshape(NX, 2, 16, 256)
-        c1.append(links.push(pw.at[k, :, 1 - c], pr.at[k], dc=1))
+    c11 = share_head(1)
+    x11 = sum_head(1, c11)
     values.done_b()
     value_head(1)
     key_sums.first_b()
-    for k in range(NY):
-        c1[k].wait_recv()
-        xs[k] = (pw[k, :, c].astype(f32) + pr[k].astype(f32)).astype(bf16)
-    x1 = [links.push(xs.at[:, lax.rem(x + k, NX)], xr.at[k - 1], dx=k) for k in (2, 1, 3)]
-    arrive(x1)
-    total = xs[:, x].astype(f32)
-    for k in range(NX - 1):
-        total = total + xr[k].astype(f32)
-    ys[...] = total.astype(bf16)
+    hand(att_ref, att_out)
+    for h, copies in ((0, x10), (1, x11)):
+        arrive(copies)
+        total = xs[h, :, x].astype(f32)
+        for k in range(NX - 1):
+            total = total + xr[h, k].astype(f32)
+        ys[:, :, head(h)] = total.astype(bf16)
     y1 = [links.push(ys.at[lax.rem(y + k, NY)], yr.at[k - 1], dy=k) for k in Y_STEPS]
+    arrive(y1)
+    total = ys[y].astype(f32)
+    for k in range(NY - 1):
+        total = total + yr[k].astype(f32)
+    sh2[...] = total.astype(bf16)
+    far = links.push(sh2, rzh, dzh=1)
+    low_rows = jnp.concatenate([lz0[...].reshape(128, DH), lz1[...].reshape(128, DH)], axis=1)
     egs[...] = dot(low_rows, wz[...].reshape(1024, 256), 1, 1).astype(bf16).reshape(NZ, 32, 1024)
     e1 = [
         links.push(egs.at[lax.rem(z + to["dz"], NZ)], egr.at[z], **to) for to in Z_PEERS
     ]
     egr[z] = egs[z]
-    arrive(y1)
-    total = ys[y].astype(f32)
-    for k in range(NY - 1):
-        total = total + yr[k].astype(f32)
-    sh2[...] = total.astype(bf16)
-    x2 = [links.push(sh2, r2.at[zh, part], **to) for to in XC_PEERS + ZH_PEERS]
-    r2[zh, part] = sh2[...]
     for h in range(2):
         query_head(h)
+    hand(qg_ref, qg_out)
     key_sums.second_a()
+    far.wait_recv()
+    sh3[...] = sh2[...].astype(f32) + rzh[...].astype(f32)
+    x2 = [links.push(sh3, r2.at[part], **to) for to in XC_PEERS]
+    r2[part] = sh3[...]
     key_sums.second_b()
     arrive(e1)
     for k in range(NZ):
-        eg_ref[0, :, k * 1024 : (k + 1) * 1024] = egr[k]
+        hand(egr.at[k], eg_out.at[0, :, k * 1024 : (k + 1) * 1024])
     kg_ref[0, :, head(0)] = (key_sums.done_a() * scale).astype(bf16)
     kg_ref[0, :, head(1)] = (key_sums.done_b() * scale).astype(bf16)
+    hand(kg_ref, kg_out)
     arrive(x2)
-    wg_ref[...] = (r2[0].astype(f32) + r2[1].astype(f32)).reshape(128, 256)
+    hand(r2, wg_out)
+    for copy in handed:
+        copy.wait()
     links.finish()
 
 
-def scatter_scratch():
+def scatter_scratch(whole):
     return [
         pltpu.VMEM((NY - 1, NZ, 32, DH), bf16),
         pltpu.VMEM((NZ - 1, NY, 32, DH), bf16),
@@ -366,21 +408,20 @@
         pltpu.VMEM((NY, 32, DH), bf16),
         pltpu.VMEM((NZ, 32, DH), f32),
         pltpu.VMEM((NY, 32, DH), f32),
-        pltpu.VMEM((NZ - 1, 32, DH), bf16),
+        pltpu.VMEM((NZ - 1, NZ, 32, DH) if whole else (NZ - 1, 32, DH), bf16),
         pltpu.VMEM((NY - 1, 32, DH), bf16),
     ]
 
 
 def hand_over(*refs):
     for i in range(5):
-        refs[5 + i][...] = refs[i][...]
+        refs[5 + i][...] = refs[i][...].reshape(refs[5 + i].shape)
 
 
 def shards(*args):
     def shape(s, t):
         return jax.ShapeDtypeStruct(s, t)
 
-    vmem = pl.BlockSpec(memory_space=pltpu.VMEM)
     pair = pltpu.VMEM((2, NZ, NY, 32, DH), bf16)
     single = pltpu.VMEM((NZ, NY, 32, DH), bf16)
     results = pl.pallas_call(
@@ -390,17 +431,21 @@
             shape((1, 512, 256), bf16),
             shape((1, 32, 256), bf16),
             shape((1, 32, 4096), bf16),
-            shape((128, 256), f32),
+            shape((8, 16, 256), f32),
         ),
         in_specs=[pl.BlockSpec(memory_space=pl.ANY)] * 8,
-        out_specs=(vmem,) * 5,
+        out_specs=(pl.BlockSpec(memory_space=pl.ANY),) * 5,
         scratch_shapes=[single] * 4
         + [pair] * 2
         + [
+            pltpu.VMEM((NX, 2, NY, 16, 256), bf16),
             pltpu.VMEM((NY, 128, 256), bf16),
             pltpu.VMEM((NZ, 32, 1024), bf16),
-            pltpu.VMEM((NZ, 32, 256), bf16),
-            pltpu.VMEM((NZ - 1, 32, 256), bf16),
+            pltpu.VMEM((NZ, 32, DH), bf16),
+            pltpu.VMEM((NZ, 32, DH), bf16),
+            pltpu.VMEM((NZ - 1, 32, DH), bf16),
+            pltpu.VMEM((NZ - 1, 32, DH), bf16),
+            pltpu.VMEM((1024, 128), bf16),
             pltpu.VMEM((NZ, 32, 1024), bf16),
             pltpu.VMEM((NZ, 32, 1024), bf16),
             pltpu.VMEM((8, BLOCK), jnp.int32),
@@ -409,17 +454,19 @@
             pltpu.VMEM((2, 512, 1024), bf16),
             pltpu.VMEM((NZ, 32, DH), bf16),
             pltpu.VMEM((NZ, 32, DH), bf16),
-            pltpu.VMEM((NY, NX, 2, 16, 256), bf16),
-            pltpu.VMEM((NY, NX, 16, 256), bf16),
-            pltpu.VMEM((NY, NX, 16, 256), bf16),
-            pltpu.VMEM((NX - 1, NY, 16, 256), bf16),
+            pltpu.VMEM((2, NY, NX, 2, 16, DH), bf16),
+            pltpu.VMEM((2, NY, NX, 16, DH), bf16),
+            pltpu.VMEM((2, NY, NX, 16, DH), bf16),
+            pltpu.VMEM((2, NX - 1, NY, 16, DH), bf16),
             pltpu.VMEM((NY, 16, 256), bf16),
             pltpu.VMEM((NY - 1, 16, 256), bf16),
             pltpu.VMEM((16, 256), bf16),
-            pltpu.VMEM((2, 8, 16, 256), bf16),
-        ]
-        + scatter_scratch()
-        + scatter_scratch()
+            pltpu.VMEM((16, 256), bf16),
+            pltpu.VMEM((16, 256), f32),
+            pltpu.VMEM((8, 16, 256), f32),
+        ]
+        + scatter_scratch(True)
+        + scatter_scratch(False)
         + [
             pltpu.VMEM((1, 512, 256), bf16),
             pltpu.VMEM((1, 32, 4096), bf16),
@@ -427,7 +474,11 @@
             pltpu.VMEM((1, 512), jnp.int32),
             pltpu.VMEM((1, 1024), jnp.int32),
             pltpu.SMEM((1, 2, 4), jnp.int32),
+            pltpu.VMEM((1, 512, 256), bf16),
+            pltpu.VMEM((1, 512, 256), bf16),
+            pltpu.VMEM((1, 32, 256), bf16),
             pltpu.SemaphoreType.DMA((10,)),
+            pltpu.SemaphoreType.DMA((8,)),
         ]
         + [pltpu.SemaphoreType.DMA((160,)), pltpu.SemaphoreType.DMA((160,))],
         compiler_params=pltpu.CompilerParams(
@@ -437,7 +488,7 @@
     )(*args[:7], jnp.swapaxes(args[7], 1, 2))
     return pl.pallas_call(
         hand_over,
-        out_shape=tuple(shape(r.shape, r.dtype) for r in results),
+        out_shape=tuple(shape(r.shape, r.dtype) for r in results[:4]) + (shape((128, 256), f32),),
         name="hand_over",
     )(*results)
 

time: 77.4 us -> 73.1 us (0.944)
  Pallas kernels: 76.6 us -> 72.3 us
    pallas_call x1, Pallas kernels: 74.5 us -> 70.2 us  [shards(): pl.pallas_call(kernel, out_shape=(shape((1, 512, 256), bf16), shape((1, 5...]
where the time goes in v3:
time: 73.1 us; the launch traced here: 73 us
  Pallas kernels  72.3 us (99%)
    pallas_call x1, Pallas kernels, shards(): pl.pallas_call(kernel, out_shape=(shape((1, 512, 256), bf16), shape((1, 5...  70.2 us
    pallas_call x1, Pallas kernels, shards(): pl.pallas_call(hand_over, out_shape=tuple((shape(r.shape, r.dtype) for r...  2.1 us

profile of v3, /device:TPU:1, one launch (start us, length us, event | category | flops | bytes accessed | tf_op | source)
XLA Modules:
  0.0 73.0 jit_solution(13051437102077044515)
XLA Ops:
  0.6 70.2 %notes.1 = (bf16[1,512,256]{2,1,0:T(8,128)(2,1)}, bf16[1,512,256]{2,1,0:T(8,128)(2,1)}, bf16[1,32,256]{2,1,0:T(8,128)(2,1)}, bf16[1,32,4096]{2,1,0:T(8,128)(2,1)}, f32[8,16,256]{2,1,0:T(8,128)}) custom-call(bf16[1,512,256]{2,1,0:T(8,128)(2,1)} %q_in.1, bf16[1,32,256]{2,1,0:T(8,128)(2,1)} %k_in.1, bf16[1,32,4096]{2,1,0:T(8,128)(2,1)} %ev_in.1, ...), custom_call_target="tpu_custom_call" | custom-call | tf_op jit(solution)/shard_map/notes/pallas_call | solution.py:427
  70.9 2.1 %hand_over.1 = (bf16[1,512,256]{2,1,0:T(8,128)(2,1)}, bf16[1,512,256]{2,1,0:T(8,128)(2,1)}, bf16[1,32,256]{2,1,0:T(8,128)(2,1)}, bf16[1,32,4096]{2,1,0:T(8,128)(2,1)}, f32[128,256]{1,0:T(8,128)}) custom-call(bf16[1,512,256]{2,1,0:T(8,128)(2,1)} %get-tuple-element.10.refs_0_, bf16[1,512,256]{2,1,0:T(8,128)(2,1)} %get-tuple-element.11.refs_1_, ...), custom_call_target="tpu_custom_call" | custom-call | tf_op jit(solution)/shard_map/hand_over/pallas_call | solution.py:489

commit v4 on v3

--- a/solution.py
+++ b/solution.py
@@ -56,6 +56,26 @@
         self.started.append(copy)
         return copy
 
+    def burst(self, whole, pushes):
+        index = self.count
+        self.count += 1
+
+        def copy(src, dst, to):
+            return pltpu.make_async_remote_copy(
+                src_ref=src,
+                dst_ref=dst,
+                send_sem=self.send_sem.at[index],
+                recv_sem=self.recv_sem.at[index],
+                device_id=device(**to),
+                device_id_type=MESH,
+            )
+
+        for src, dst, to in pushes:
+            copy(src, dst, to).start()
+        total = copy(whole, whole, dict(dc=1))
+        self.started.append(total)
+        return [total]
+
     def fetch(self, src, dst, sem):
         copy = pltpu.make_async_copy(src, dst, sem)
         copy.start()
@@ -82,20 +102,30 @@
 
     def first_a(self):
         z, y, buf = self.z, self.y, self.buf
-        self.a1 = [self.links.push(buf[0].at[z, y], buf[0].at[z, y], **to) for to in Z_PEERS]
+        self.a1 = self.links.burst(
+            buf[0].at[0, pl.ds(0, 3)], [(buf[0].at[z, y], buf[0].at[z, y], to) for to in Z_PEERS]
+        )
 
     def first_b(self):
         z, y, buf = self.z, self.y, self.buf
-        self.b1 = [self.links.push(buf[1].at[z, y], buf[1].at[z, y], dy=k) for k in Y_STEPS]
+        self.b1 = self.links.burst(
+            buf[1].at[0, pl.ds(0, 7)],
+            [(buf[1].at[z, y], buf[1].at[z, y], dict(dy=k)) for k in Y_STEPS],
+        )
 
     def second_a(self):
         y, buf = self.y, self.buf
-        self.a2 = [self.links.push(buf[0].at[:, y], buf[0].at[:, y], dy=k) for k in Y_STEPS]
+        self.a2 = self.links.burst(
+            buf[0].at[:, pl.ds(0, 7)],
+            [(buf[0].at[:, y], buf[0].at[:, y], dict(dy=k)) for k in Y_STEPS],
+        )
 
     def second_b(self):
         arrive(self.b1)
         z, buf = self.z, self.buf
-        self.b2 = [self.links.push(buf[1].at[z], buf[1].at[z], **to) for to in Z_PEERS]
+        self.b2 = self.links.burst(
+            buf[1].at[pl.ds(0, 3)], [(buf[1].at[z], buf[1].at[z], to) for to in Z_PEERS]
+        )
 
     def done_a(self):
         arrive(self.a2)
@@ -111,18 +141,22 @@
         self.z, self.y = place()[:2]
 
     def first_a(self):
-        self.a1 = [
-            self.links.push(self.src.at[0, :, lax.rem(self.y + k, NY)], self.ra1.at[k - 1], dy=k)
-            for k in Y_STEPS
-        ]
+        self.a1 = self.links.burst(
+            self.ra1,
+            [
+                (self.src.at[0, :, lax.rem(self.y + k, NY)], self.ra1.at[k - 1], dict(dy=k))
+                for k in Y_STEPS
+            ],
+        )
 
     def first_b(self):
-        self.b1 = [
-            self.links.push(
-                self.src.at[1, lax.rem(self.z + to["dz"], NZ)], self.rb1.at[to["dz"] - 1], **to
-            )
-            for to in Z_PEERS
-        ]
+        self.b1 = self.links.burst(
+            self.rb1,
+            [
+                (self.src.at[1, lax.rem(self.z + to["dz"], NZ)], self.rb1.at[to["dz"] - 1], to)
+                for to in Z_PEERS
+            ],
+        )
 
     def second_a(self, whole=False):
         arrive(self.a1)
@@ -131,14 +165,17 @@
             total = total + self.ra1[k].astype(f32)
         self.fa[...] = total
         self.sa[...] = total.astype(bf16)
-        self.a2 = [
-            self.links.push(
-                self.sa if whole else self.sa.at[lax.rem(self.z + to["dz"], NZ)],
-                self.ra2.at[to["dz"] - 1],
-                **to,
-            )
-            for to in Z_PEERS
-        ]
+        self.a2 = self.links.burst(
+            self.ra2,
+            [
+                (
+                    self.sa if whole else self.sa.at[lax.rem(self.z + to["dz"], NZ)],
+                    self.ra2.at[to["dz"] - 1],
+                    to,
+                )
+                for to in Z_PEERS
+            ],
+        )
 
     def second_b(self):
         arrive(self.b1)
@@ -147,10 +184,13 @@
             total = total + self.rb1[k].astype(f32)
         self.fb[...] = total
         self.sb[...] = total.astype(bf16)
-        self.b2 = [
-            self.links.push(self.sb.at[lax.rem(self.y + k, NY)], self.rb2.at[k - 1], dy=k)
-            for k in Y_STEPS
-        ]
+        self.b2 = self.links.burst(
+            self.rb2,
+            [
+                (self.sb.at[lax.rem(self.y + k, NY)], self.rb2.at[k - 1], dict(dy=k))
+                for k in Y_STEPS
+            ],
+        )
 
     def done_a(self, whole=False):
         arrive(self.a2)
@@ -206,7 +246,10 @@
     pl.semaphore_wait(barrier, len(peers))
     for load in loads[2:4]:
         load.wait()
-    w1 = [links.push(wq.at[x, c, y], wq.at[x, c, y], dy=k) for k in Y_STEPS]
+    w1 = links.burst(
+        wq.at[0, 0, pl.ds(0, 7)],
+        [(wq.at[x, c, y], wq.at[x, c, y], dict(dy=k)) for k in Y_STEPS],
+    )
     for load in loads[:2]:
         load.wait()
     keys = Gather(links, kall)
@@ -215,7 +258,8 @@
     ev1 = []
     for to in Z_PEERS:
         there = pl.ds(pl.multiple_of(lax.rem(z + to["dz"], NZ) * 1024, 1024), 1024)
-        ev1.append(links.push(ev_ref.at[0, :, there], evz.at[z], **to))
+        ev1.append((ev_ref.at[0, :, there], evz.at[z], to))
+    ev1 = links.burst(evz.at[pl.ds(0, 3)], ev1)
     for load in loads[4:]:
         load.wait()
     for e in range(8):
@@ -240,12 +284,20 @@
     partial = dot(evz[...].reshape(128, 1024), wz[...].reshape(1024, 256), 1, 0)
     pz0[...] = partial[:, :DH].reshape(NZ, 32, DH).astype(bf16)
     pz1[...] = partial[:, DH:].reshape(NZ, 32, DH).astype(bf16)
-    z1a = [
-        links.push(pz0.at[lax.rem(z + to["dz"], NZ)], rz0.at[to["dz"] - 1], **to) for to in Z_PEERS
-    ]
-    z1b = [
-        links.push(pz1.at[lax.rem(z + to["dz"], NZ)], rz1.at[to["dz"] - 1], **to) for to in Z_PEERS
-    ]
+    z1a = links.burst(
+        rz0,
+        [
+            (pz0.at[lax.rem(z + to["dz"], NZ)], rz0.at[to["dz"] - 1], to)
+            for to in Z_PEERS
+        ],
+    )
+    z1b = links.burst(
+        rz1,
+        [
+            (pz1.at[lax.rem(z + to["dz"], NZ)], rz1.at[to["dz"] - 1], to)
+            for to in Z_PEERS
+        ],
+    )
     patients = []
     for n in range(notes):
         row = np_ref[:, n * BLOCK : (n + 1) * BLOCK]
@@ -277,9 +329,13 @@
     def sum_head(h, copy):
         copy.wait_recv()
         xs[h] = (pw[h, :, :, c].astype(f32) + pr[h].astype(f32)).astype(bf16)
-        return [
-            links.push(xs.at[h, :, lax.rem(x + k, NX)], xr.at[h, k - 1], dx=k) for k in (2, 1, 3)
-        ]
+        return links.burst(
+            xr.at[h],
+            [
+                (xs.at[h, :, lax.rem(x + k, NX)], xr.at[h, k - 1], dict(dx=k))
+                for k in (2, 1, 3)
+            ],
+        )
 
     def score_head(h):
         for n in range(notes):
@@ -345,7 +401,7 @@
     values.second_a()
     values.second_b()
     lz1[z] = value_sums.done_b().astype(bf16)
-    low1 = [links.push(lz1.at[z], lz1.at[z], **to) for to in Z_PEERS]
+    low1 = links.burst(lz1.at[pl.ds(0, 3)], [(lz1.at[z], lz1.at[z], to) for to in Z_PEERS])
     lz0[...] = value_sums.done_a(whole=True).astype(bf16)
     c10 = share_head(0)
     x10 = sum_head(0, c10)
@@ -365,7 +421,12 @@
         for k in range(NX - 1):
             total = total + xr[h, k].astype(f32)
         ys[:, :, head(h)] = total.astype(bf16)
-    y1 = [links.push(ys.at[lax.rem(y + k, NY)], yr.at[k - 1], dy=k) for k in Y_STEPS]
+    y1 = links.burst(
+        yr, [(ys.at[lax.rem(y + k, NY)], yr.at[k - 1], dict(dy=k)) for k in Y_STEPS]
+    )
+    for h in range(2):
+        query_head(h)
+    hand(qg_ref, qg_out)
     arrive(y1)
     total = ys[y].astype(f32)
     for k in range(NY - 1):
@@ -374,17 +435,15 @@
     far = links.push(sh2, rzh, dzh=1)
     low_rows = jnp.concatenate([lz0[...].reshape(128, DH), lz1[...].reshape(128, DH)], axis=1)
     egs[...] = dot(low_rows, wz[...].reshape(1024, 256), 1, 1).astype(bf16).reshape(NZ, 32, 1024)
-    e1 = [
-        links.push(egs.at[lax.rem(z + to["dz"], NZ)], egr.at[z], **to) for to in Z_PEERS
-    ]
+    e1 = links.burst(
+        egr.at[pl.ds(0, 3)],
+        [(egs.at[lax.rem(z + to["dz"], NZ)], egr.at[z], to) for to in Z_PEERS],
+    )
     egr[z] = egs[z]
-    for h in range(2):
-        query_head(h)
-    hand(qg_ref, qg_out)
     key_sums.second_a()
     far.wait_recv()
     sh3[...] = sh2[...].astype(f32) + rzh[...].astype(f32)
-    x2 = [links.push(sh3, r2.at[part], **to) for to in XC_PEERS]
+    x2 = links.burst(r2.at[pl.ds(0, 7)], [(sh3, r2.at[part], to) for to in XC_PEERS])
     r2[part] = sh3[...]
     key_sums.second_b()
     arrive(e1)
@@ -480,7 +539,7 @@
             pltpu.SemaphoreType.DMA((10,)),
             pltpu.SemaphoreType.DMA((8,)),
         ]
-        + [pltpu.SemaphoreType.DMA((160,)), pltpu.SemaphoreType.DMA((160,))],
+        + [pltpu.SemaphoreType.DMA((36,)), pltpu.SemaphoreType.DMA((36,))],
         compiler_params=pltpu.CompilerParams(
             collective_id=0, has_side_effects=True, vmem_limit_bytes=60 * 1024 * 1024
         ),

time: 73.1 us -> 70.5 us (0.964)
  Pallas kernels: 72.3 us -> 69.7 us
    pallas_call x1, Pallas kernels: 70.2 us -> 67.6 us  [shards(): pl.pallas_call(kernel, out_shape=(shape((1, 512, 256), bf16), shape((1, 5...]
where the time goes in v4:
time: 70.5 us; the launch traced here: 70.3 us
  Pallas kernels  69.7 us (99%)
    pallas_call x1, Pallas kernels, shards(): pl.pallas_call(kernel, out_shape=(shape((1, 512, 256), bf16), shape((1, 5...  67.6 us
    pallas_call x1, Pallas kernels, shards(): pl.pallas_call(hand_over, out_shape=tuple((shape(r.shape, r.dtype) for r...  2.1 us

profile of v4, /device:TPU:1, one launch (start us, length us, event | category | flops | bytes accessed | tf_op | source)
XLA Modules:
  0.0 70.3 jit_solution(725571902436536486)
XLA Ops:
  0.6 67.6 %notes.1 = (bf16[1,512,256]{2,1,0:T(8,128)(2,1)}, bf16[1,512,256]{2,1,0:T(8,128)(2,1)}, bf16[1,32,256]{2,1,0:T(8,128)(2,1)}, bf16[1,32,4096]{2,1,0:T(8,128)(2,1)}, f32[8,16,256]{2,1,0:T(8,128)}) custom-call(bf16[1,512,256]{2,1,0:T(8,128)(2,1)} %q_in.1, bf16[1,32,256]{2,1,0:T(8,128)(2,1)} %k_in.1, bf16[1,32,4096]{2,1,0:T(8,128)(2,1)} %ev_in.1, ...), custom_call_target="tpu_custom_call" | custom-call | tf_op jit(solution)/shard_map/notes/pallas_call | solution.py:486
  68.2 2.1 %hand_over.1 = (bf16[1,512,256]{2,1,0:T(8,128)(2,1)}, bf16[1,512,256]{2,1,0:T(8,128)(2,1)}, bf16[1,32,256]{2,1,0:T(8,128)(2,1)}, bf16[1,32,4096]{2,1,0:T(8,128)(2,1)}, f32[128,256]{1,0:T(8,128)}) custom-call(bf16[1,512,256]{2,1,0:T(8,128)(2,1)} %get-tuple-element.10.refs_0_, bf16[1,512,256]{2,1,0:T(8,128)(2,1)} %get-tuple-element.11.refs_1_, ...), custom_call_target="tpu_custom_call" | custom-call | tf_op jit(solution)/shard_map/hand_over/pallas_call | solution.py:548

commit v5 on v4

--- a/solution.py
+++ b/solution.py
@@ -443,8 +443,9 @@
     key_sums.second_a()
     far.wait_recv()
     sh3[...] = sh2[...].astype(f32) + rzh[...].astype(f32)
-    x2 = links.burst(r2.at[pl.ds(0, 7)], [(sh3, r2.at[part], to) for to in XC_PEERS])
-    r2[part] = sh3[...]
+    mine = pl.ds(pl.multiple_of(part * 16, 16), 16)
+    x2 = links.burst(r2.at[pl.ds(0, 112)], [(sh3, r2.at[mine], to) for to in XC_PEERS])
+    r2[mine] = sh3[...]
     key_sums.second_b()
     arrive(e1)
     for k in range(NZ):
@@ -473,8 +474,16 @@
 
 
 def hand_over(*refs):
+    held, sem = refs[10:15], refs[15]
+    inward = [pltpu.make_async_copy(refs[i], held[i], sem.at[i]) for i in range(5)]
+    outward = [pltpu.make_async_copy(held[i], refs[5 + i], sem.at[5 + i]) for i in range(5)]
+    for copy in inward:
+        copy.start()
     for i in range(5):
-        refs[5 + i][...] = refs[i][...].reshape(refs[5 + i].shape)
+        inward[i].wait()
+        outward[i].start()
+    for copy in outward:
+        copy.wait()
 
 
 def shards(*args):
@@ -490,7 +499,7 @@
             shape((1, 512, 256), bf16),
             shape((1, 32, 256), bf16),
             shape((1, 32, 4096), bf16),
-            shape((8, 16, 256), f32),
+            shape((128, 256), f32),
         ),
         in_specs=[pl.BlockSpec(memory_space=pl.ANY)] * 8,
         out_specs=(pl.BlockSpec(memory_space=pl.ANY),) * 5,
@@ -522,7 +531,7 @@
             pltpu.VMEM((16, 256), bf16),
             pltpu.VMEM((16, 256), bf16),
             pltpu.VMEM((16, 256), f32),
-            pltpu.VMEM((8, 16, 256), f32),
+            pltpu.VMEM((128, 256), f32),
         ]
         + scatter_scratch(True)
         + scatter_scratch(False)
@@ -547,7 +556,12 @@
     )(*args[:7], jnp.swapaxes(args[7], 1, 2))
     return pl.pallas_call(
         hand_over,
-        out_shape=tuple(shape(r.shape, r.dtype) for r in results[:4]) + (shape((128, 256), f32),),
+        out_shape=tuple(shape(r.shape, r.dtype) for r in results),
+        in_specs=[pl.BlockSpec(memory_space=pl.ANY)] * 5,
+        out_specs=(pl.BlockSpec(memory_space=pl.ANY),) * 5,
+        scratch_shapes=[pltpu.VMEM(r.shape, r.dtype) for r in results]
+        + [pltpu.SemaphoreType.DMA((10,))],
+        compiler_params=pltpu.CompilerParams(vmem_limit_bytes=60 * 1024 * 1024),
         name="hand_over",
     )(*results)
 

time: 70.5 us -> 70.3 us (level)
  no operation moved by 1% of the time
where the time goes in v5:
time: 70.3 us; the launch traced here: 70.2 us
  Pallas kernels  69.6 us (99%)
    pallas_call x1, Pallas kernels, shards(): pl.pallas_call(kernel, out_shape=(shape((1, 512, 256), bf16), shape((1, 5...  67.6 us
    pallas_call x1, Pallas kernels, shards(): pl.pallas_call(hand_over, out_shape=tuple((shape(r.shape, r.dtype) for r...  1.96 us

profile of v5, /device:TPU:1, one launch (start us, length us, event | category | flops | bytes accessed | tf_op | source)
XLA Modules:
  0.0 70.2 jit_solution(13196787285331191168)
XLA Ops:
  0.6 67.6 %notes.1 = (bf16[1,512,256]{2,1,0:T(8,128)(2,1)}, bf16[1,512,256]{2,1,0:T(8,128)(2,1)}, bf16[1,32,256]{2,1,0:T(8,128)(2,1)}, bf16[1,32,4096]{2,1,0:T(8,128)(2,1)}, f32[128,256]{1,0:T(8,128)}) custom-call(bf16[1,512,256]{2,1,0:T(8,128)(2,1)} %q_in.1, bf16[1,32,256]{2,1,0:T(8,128)(2,1)} %k_in.1, bf16[1,32,4096]{2,1,0:T(8,128)(2,1)} %ev_in.1, ...), custom_call_target="tpu_custom_call" | custom-call | tf_op jit(solution)/shard_map/notes/pallas_call | solution.py:495
  68.2 2.0 %hand_over.1 = (bf16[1,512,256]{2,1,0:T(8,128)(2,1)}, bf16[1,512,256]{2,1,0:T(8,128)(2,1)}, bf16[1,32,256]{2,1,0:T(8,128)(2,1)}, bf16[1,32,4096]{2,1,0:T(8,128)(2,1)}, f32[128,256]{1,0:T(8,128)}) custom-call(bf16[1,512,256]{2,1,0:T(8,128)(2,1)} %get-tuple-element.10.refs_0_, bf16[1,512,256]{2,1,0:T(8,128)(2,1)} %get-tuple-element.11.refs_1_, ...), custom_call_target="tpu_custom_call" | custom-call | tf_op jit(solution)/shard_map/hand_over/pallas_call | solution.py:557
